TPU v7x, 256 devices: a whole 4x4x8 slice. The times are simulated.
256 devices in a mesh: tmpl: 4 (over y_lo, core), row: 64 (over z, y_hi, x).
Axes of the slice: x: 4, y: 4 (y_hi: 2, y_lo: 2; y = y_hi * 2 + y_lo), z: 8, core: 2. Of those that a mesh axis runs over, the one named last changes fastest.
Arguments:
- saved_out: bfloat16 [4, 64, 512, 512], P('tmpl', None, 'row'), may hold values from -6 to 6
- sum_out: bfloat16 [4, 64, 512, 512], P('tmpl', None, 'row'), may hold values from -135 to 135
- saved_in: bfloat16 [4, 64, 512, 512], P('tmpl', None, 'row'), may hold values from -6 to 6
- sum_in: bfloat16 [4, 64, 512, 512], P('tmpl', None, 'row'), may hold values from -135 to 135
- cotangent: bfloat16 [4, 64, 512, 512], P('tmpl', None, 'row'), may hold values from -6 to 6
- w_in: bfloat16 [2, 64, 320], replicated, may hold values from -0.75 to 0.75
- w_out: bfloat16 [2, 64, 64], replicated, may hold values from -0.75 to 0.75
- norm_gain: float32 [2, 2, 64], replicated, may hold values from 0.5 to 1.5
- norm_shift: float32 [2, 2, 64], replicated, may hold values from -3 to 3
Outputs:
- grad_trunk: bfloat16 [64, 512, 512], P(None, 'row', 'tmpl')
- grad_w_in: float32 [2, 64, 320], replicated
- grad_w_out: float32 [2, 64, 64], replicated
- grad_gain: float32 [2, 2, 64], replicated
- grad_shift: float32 [2, 2, 64], replicated
All inputs are finite; a program needn't handle non-finite values.
Results may differ from a plain program's by a relative error of at most 0.015.
Values may be sent and summed in bfloat16 or wider, within the bound.
A program may use at most 64 MiB of HBM per device.

v0:
```python
import jax
import jax.numpy as jnp
from jax import lax
from jax.sharding import PartitionSpec as P

EPSILON = 1e-05


def norm_forward(values, gain_vec, shift_vec):
    average = jnp.mean(values, axis=0)
    centred = values - average
    variance = jnp.mean(centred * centred, axis=0)
    inv_dev = lax.rsqrt(variance + EPSILON)
    standard = centred * inv_dev
    return (standard, inv_dev, standard * gain_vec[:, None, None] + shift_vec[:, None, None])


def norm_backward(grad_in, standard, inv_dev, gain_vec):
    scaled = grad_in * gain_vec[:, None, None]
    return inv_dev * (
        scaled - jnp.mean(scaled, axis=0) - standard * jnp.mean(scaled * standard, axis=0)
    )


def prepare(saved, saved_sum, gains, shifts, weight_in, weight_out):
    channels = weight_out.shape[0]
    standard, inv_dev, normed = norm_forward(saved.astype(jnp.float32), gains[0], shifts[0])
    normed_b = normed.astype(jnp.bfloat16)
    projected = jnp.einsum("cf,crn->frn", weight_in, normed_b, preferred_element_type=jnp.float32)
    gate_a = jax.nn.sigmoid(projected[:channels])
    pair_a = (gate_a * projected[channels : 2 * channels]).astype(jnp.bfloat16)
    gate_b = jax.nn.sigmoid(projected[2 * channels : 3 * channels])
    pair_b = (gate_b * projected[3 * channels : 4 * channels]).astype(jnp.bfloat16)
    gate_out = jax.nn.sigmoid(projected[4 * channels :])
    sum_standard, sum_inv, normed_two = norm_forward(
        saved_sum.astype(jnp.float32), gains[1], shifts[1]
    )
    normed_two_b = normed_two.astype(jnp.bfloat16)
    update = jnp.einsum("cd,crn->drn", weight_out, normed_two_b, preferred_element_type=jnp.float32)
    return (
        standard,
        inv_dev,
        normed_b,
        projected,
        pair_a,
        pair_b,
        gate_out,
        sum_standard,
        sum_inv,
        normed_two_b,
        update,
    )


def head_backward(state, upstream, gains, weight_out):
    gate_out = state[6]
    gated_cotan = (gate_out * upstream).astype(jnp.bfloat16)
    d_gate = upstream * state[10]
    grad_out = jnp.einsum("crn,drn->cd", state[9], gated_cotan, preferred_element_type=jnp.float32)
    d_normed_two = jnp.einsum(
        "cd,drn->crn", weight_out, gated_cotan, preferred_element_type=jnp.float32
    )
    gain_two = jnp.sum(d_normed_two * state[7], axis=(1, 2))
    shift_two = jnp.sum(d_normed_two, axis=(1, 2))
    d_sum = norm_backward(d_normed_two, state[7], state[8], gains[1]).astype(jnp.bfloat16)
    return (d_sum, d_gate, grad_out, gain_two, shift_two)


def tail_backward(state, d_pair_a, d_pair_b, d_gate, gains, weight_in):
    channels = weight_in.shape[0]
    projected = state[3]
    gate_a = jax.nn.sigmoid(projected[:channels])
    value_a = projected[channels : 2 * channels]
    gate_b = jax.nn.sigmoid(projected[2 * channels : 3 * channels])
    value_b = projected[3 * channels : 4 * channels]
    gate_out = state[6]
    grad_a = d_pair_a.astype(jnp.float32)
    grad_b = d_pair_b.astype(jnp.float32)
    d_projected = jnp.concatenate(
        [
            grad_a * value_a * gate_a * (1.0 - gate_a),
            grad_a * gate_a,
            grad_b * value_b * gate_b * (1.0 - gate_b),
            grad_b * gate_b,
            d_gate * gate_out * (1.0 - gate_out),
        ],
        axis=0,
    ).astype(jnp.bfloat16)
    grad_in = jnp.einsum("crn,frn->cf", state[2], d_projected, preferred_element_type=jnp.float32)
    d_normed = jnp.einsum("cf,frn->crn", weight_in, d_projected, preferred_element_type=jnp.float32)
    gain_one = jnp.sum(d_normed * state[0], axis=(1, 2))
    shift_one = jnp.sum(d_normed, axis=(1, 2))
    d_saved = norm_backward(d_normed, state[0], state[1], gains[0])
    return (d_saved, grad_in, gain_one, shift_one)


def triangle(d_sum, pair_a, pair_b, outgoing):
    if outgoing:
        grad_a = jnp.einsum("hij,hjk->hik", d_sum, pair_b, preferred_element_type=jnp.float32)
        grad_b = jnp.einsum("hij,hik->hjk", d_sum, pair_a, preferred_element_type=jnp.float32)
    else:
        grad_a = jnp.einsum("hkj,hij->hki", pair_b, d_sum, preferred_element_type=jnp.float32)
        grad_b = jnp.einsum("hki,hij->hkj", pair_a, d_sum, preferred_element_type=jnp.float32)
    return (grad_a.astype(jnp.bfloat16), grad_b.astype(jnp.bfloat16))


def send_back(grad_a, grad_b):
    return (
        lax.all_to_all(grad_a, "row", split_axis=1, concat_axis=0, tiled=True),
        lax.all_to_all(grad_b, "row", split_axis=1, concat_axis=0, tiled=True),
    )


def finish(state, upstream, head_parts, spread_dx, spread_a, spread_b, gains, weight_in, outgoing):
    tri_a, tri_b = triangle(spread_dx, spread_a, spread_b, outgoing)
    local_parts = send_back(tri_a, tri_b)
    tails = tail_backward(state, local_parts[0], local_parts[1], head_parts[1], gains, weight_in)
    grads = (
        tails[1],
        head_parts[2],
        jnp.stack([tails[2], head_parts[3]]),
        jnp.stack([tails[3], head_parts[4]]),
    )
    return (upstream + tails[0], grads)


def shards(saved_out, sum_out, saved_in, sum_in, cotangent, w_in, w_out, norm_gain, norm_shift):
    state_in = prepare(saved_in[0], sum_in[0], norm_gain[1], norm_shift[1], w_in[1], w_out[1])
    upstream_in = cotangent[0].astype(jnp.float32)
    head_in = head_backward(state_in, upstream_in, norm_gain[1], w_out[1])
    state_out = prepare(saved_out[0], sum_out[0], norm_gain[0], norm_shift[0], w_in[0], w_out[0])
    early_parts = (
        lax.all_to_all(head_in[0], "row", split_axis=0, concat_axis=1, tiled=True),
        lax.all_to_all(state_in[4], "row", split_axis=0, concat_axis=1, tiled=True),
        lax.all_to_all(state_in[5], "row", split_axis=0, concat_axis=1, tiled=True),
    )
    upstream_out, grads_in = finish(
        state_in,
        upstream_in,
        head_in,
        early_parts[0],
        early_parts[1],
        early_parts[2],
        norm_gain[1],
        w_in[1],
        False,
    )
    head_out = head_backward(state_out, upstream_out, norm_gain[0], w_out[0])
    late_parts = (
        lax.all_to_all(head_out[0], "row", split_axis=0, concat_axis=1, tiled=True),
        lax.all_to_all(state_out[4], "row", split_axis=0, concat_axis=1, tiled=True),
        lax.all_to_all(state_out[5], "row", split_axis=0, concat_axis=1, tiled=True),
    )
    spread_dx = late_parts[0]
    outer_a = late_parts[1]
    outer_b = late_parts[2]
    result_trunk, grads_out = finish(
        state_out, upstream_out, head_out, spread_dx, outer_a, outer_b, norm_gain[0], w_in[0], True
    )
    stacked = tuple(
        (jnp.stack([first_dir, second_dir]) for first_dir, second_dir in zip(grads_out, grads_in))
    )
    summed = lax.psum(stacked, ("tmpl", "row"))
    grad_trunk = lax.psum_scatter(
        result_trunk.astype(jnp.bfloat16), "tmpl", scatter_dimension=2, tiled=True
    )
    templates = lax.axis_size("tmpl")
    residues = saved_out.shape[3]
    factor = 1.0 / (templates * residues)
    return (
        grad_trunk,
        summed[0] * factor,
        summed[1] * factor,
        summed[2] * factor,
        summed[3] * factor,
    )


def solution(mesh):
    in_specs = (
        P("tmpl", None, "row", None),
        P("tmpl", None, "row", None),
        P("tmpl", None, "row", None),
        P("tmpl", None, "row", None),
        P("tmpl", None, "row", None),
        P(),
        P(),
        P(),
        P(),
    )
    out_specs = (P(None, "row", "tmpl"), P(), P(), P(), P())
    return jax.shard_map(shards, mesh=mesh, in_specs=in_specs, out_specs=out_specs, check_vma=False)
```

profile of v0, /device:TPU:1, one launch (start us, length us, event | category | flops | bytes accessed | tf_op | source)
XLA Modules:
  0.0 551.0 jit_solution(4766076175284304177)
XLA Ops:
  16.9 15.1 %all-to-all-start = ((bf16[64,8,512]{2,1,0:T(8,128)(2,1)}), bf16[64,8,512]{2,1,0:T(8,128)(2,1)S(1)}, u32[]{:S(2)}, u32[]{:S(2)}) async-start(bf16[64,8,512]{2,1,0:T(8,128)(2,1)} %copy.45), calls=%async_computation | async-start | bytes 1048576 | tf_op jit(solution)/shard_map/all_to_all | solution.py:135
  35.3 12.6 %all-to-all-done = bf16[64,8,512]{2,1,0:T(8,128)(2,1)S(1)} async-done(((bf16[64,8,512]{2,1,0:T(8,128)(2,1)}), bf16[64,8,512]{2,1,0:T(8,128)(2,1)S(1)}, u32[]{:S(2)}, u32[]{:S(2)}) %all-to-all-start) | async-done | bytes 524320 | tf_op jit(solution)/shard_map/all_to_all | solution.py:135
  47.9 8.4 %all-to-all-start.1 = ((bf16[64,8,512]{2,1,0:T(8,128)(2,1)}), bf16[64,8,512]{2,1,0:T(8,128)(2,1)S(1)}, u32[]{:S(2)}, u32[]{:S(2)}) async-start(bf16[64,8,512]{2,1,0:T(8,128)(2,1)} %copy.47), calls=%async_computation.1 | async-start | bytes 1048576 | tf_op jit(solution)/shard_map/all_to_all | solution.py:133
  57.3 13.6 %all-to-all-done.1 = bf16[64,8,512]{2,1,0:T(8,128)(2,1)S(1)} async-done(((bf16[64,8,512]{2,1,0:T(8,128)(2,1)}), bf16[64,8,512]{2,1,0:T(8,128)(2,1)S(1)}, u32[]{:S(2)}, u32[]{:S(2)}) %all-to-all-start.1) | async-done | bytes 524320 | tf_op jit(solution)/shard_map/all_to_all | solution.py:133
  70.9 9.6 %all-to-all-start.3 = ((bf16[64,8,512]{2,1,0:T(8,128)(2,1)}), bf16[64,8,512]{2,1,0:T(8,128)(2,1)}, u32[]{:S(2)}, u32[]{:S(2)}) async-start(bf16[64,8,512]{2,1,0:T(8,128)(2,1)} %copy.52), calls=%async_computation.3 | async-start | bytes 1048576 | tf_op jit(solution)/shard_map/all_to_all | solution.py:134
  87.1 7.6 %all-to-all-done.3 = bf16[64,8,512]{2,1,0:T(8,128)(2,1)} async-done(((bf16[64,8,512]{2,1,0:T(8,128)(2,1)}), bf16[64,8,512]{2,1,0:T(8,128)(2,1)}, u32[]{:S(2)}, u32[]{:S(2)}) %all-to-all-start.3) | async-done | bytes 524320 | tf_op jit(solution)/shard_map/all_to_all | solution.py:134
  94.8 9.7 %all-to-all-start.2 = ((bf16[64,2,2048]{2,1,0:T(2,128)(2,1)}), bf16[64,2,2048]{2,1,0:T(2,128)(2,1)}, u32[]{:S(2)}, u32[]{:S(2)}) async-start(bf16[64,2,2048]{2,1,0:T(2,128)(2,1)} %reshape.195), calls=%async_computation.2 | async-start | bytes 1048576 | tf_op jit(solution)/shard_map/all_to_all | solution.py:109
  112.0 6.7 %all-to-all-done.2 = bf16[64,2,2048]{2,1,0:T(2,128)(2,1)} async-done(((bf16[64,2,2048]{2,1,0:T(2,128)(2,1)}), bf16[64,2,2048]{2,1,0:T(2,128)(2,1)}, u32[]{:S(2)}, u32[]{:S(2)}) %all-to-all-start.2) | async-done | bytes 524320 | tf_op jit(solution)/shard_map/all_to_all | solution.py:109
  118.7 9.8 %all-to-all-start.4 = ((bf16[64,2,2048]{2,1,0:T(2,128)(2,1)}), bf16[64,2,2048]{2,1,0:T(2,128)(2,1)S(1)}, u32[]{:S(2)}, u32[]{:S(2)}) async-start(bf16[64,2,2048]{2,1,0:T(2,128)(2,1)} %reshape.197), calls=%async_computation.4 | async-start | bytes 1048576 | tf_op jit(solution)/shard_map/all_to_all | solution.py:110
  132.3 4.5 reshape.196
  138.2 4.7 all-to-all-done.4
  159.2 9.7 %all-to-all-start.6 = ((bf16[64,8,512]{2,1,0:T(8,128)(2,1)}), bf16[64,8,512]{2,1,0:T(8,128)(2,1)}, u32[]{:S(2)}, u32[]{:S(2)}) async-start(bf16[64,8,512]{2,1,0:T(8,128)(2,1)} %copy.61), calls=%async_computation.6 | async-start | bytes 1048576 | tf_op jit(solution)/shard_map/all_to_all | solution.py:152
  174.4 8.8 %all-to-all-done.6 = bf16[64,8,512]{2,1,0:T(8,128)(2,1)} async-done(((bf16[64,8,512]{2,1,0:T(8,128)(2,1)}), bf16[64,8,512]{2,1,0:T(8,128)(2,1)}, u32[]{:S(2)}, u32[]{:S(2)}) %all-to-all-start.6) | async-done | bytes 524320 | tf_op jit(solution)/shard_map/all_to_all | solution.py:152
  183.2 9.8 %all-to-all-start.5 = ((bf16[64,8,512]{2,1,0:T(8,128)(2,1)}), bf16[64,8,512]{2,1,0:T(8,128)(2,1)}, u32[]{:S(2)}, u32[]{:S(2)}) async-start(bf16[64,8,512]{2,1,0:T(8,128)(2,1)} %copy.60), calls=%async_computation.5 | async-start | bytes 1048576 | tf_op jit(solution)/shard_map/all_to_all | solution.py:150
  195.1 12.1 %all-to-all-done.5 = bf16[64,8,512]{2,1,0:T(8,128)(2,1)} async-done(((bf16[64,8,512]{2,1,0:T(8,128)(2,1)}), bf16[64,8,512]{2,1,0:T(8,128)(2,1)}, u32[]{:S(2)}, u32[]{:S(2)}) %all-to-all-start.5) | async-done | bytes 524320 | tf_op jit(solution)/shard_map/all_to_all | solution.py:150
  207.3 9.7 %all-to-all-start.8 = ((bf16[64,8,512]{2,1,0:T(8,128)(2,1)}), bf16[64,8,512]{2,1,0:T(8,128)(2,1)}, u32[]{:S(2)}, u32[]{:S(2)}) async-start(bf16[64,8,512]{2,1,0:T(8,128)(2,1)} %copy.66), calls=%async_computation.8 | async-start | bytes 1048576 | tf_op jit(solution)/shard_map/all_to_all | solution.py:151
  231.2 9.6 %all-to-all-start.7 = ((bf16[64,2,2048]{2,1,0:T(2,128)(2,1)}), bf16[64,2,2048]{2,1,0:T(2,128)(2,1)S(1)}, u32[]{:S(2)}, u32[]{:S(2)}) async-start(bf16[64,2,2048]{2,1,0:T(2,128)(2,1)} %reshape.199), calls=%async_computation.7 | async-start | bytes 1048576 | tf_op jit(solution)/shard_map/all_to_all | solution.py:109
  243.4 4.6 reduce.11
  250.2 4.7 all-to-all-done.7
  254.9 9.6 %all-to-all-start.9 = ((bf16[64,2,2048]{2,1,0:T(2,128)(2,1)}), bf16[64,2,2048]{2,1,0:T(2,128)(2,1)}, u32[]{:S(2)}, u32[]{:S(2)}) async-start(bf16[64,2,2048]{2,1,0:T(2,128)(2,1)} %reshape.201), calls=%async_computation.9 | async-start | bytes 1048576 | tf_op jit(solution)/shard_map/all_to_all | solution.py:110
  272.2 6.2 %all-to-all-done.9 = bf16[64,2,2048]{2,1,0:T(2,128)(2,1)} async-done(((bf16[64,2,2048]{2,1,0:T(2,128)(2,1)}), bf16[64,2,2048]{2,1,0:T(2,128)(2,1)}, u32[]{:S(2)}, u32[]{:S(2)}) %all-to-all-start.9) | async-done | bytes 524320 | tf_op jit(solution)/shard_map/all_to_all | solution.py:110
  278.3 4.4 reshape.202
  296.5 79.3 %all-reduce = (f32[2,64,64]{2,1,0:T(8,128)S(1)}, f32[2,2,64]{2,1,0:T(2,128)S(1)}, f32[2,2,64]{2,1,0:T(2,128)S(1)}) all-reduce(f32[2,64,64]{2,1,0:T(8,128)S(1)} %pad_maximum_fusion.1, f32[2,2,64]{2,1,0:T(2,128)S(1)} %pad_maximum_fusion.2, f32[2,2,64]{2,1,0:T(2,128)S(1)} %pad_maximum_fusion.3), channel_id=1, replica_groups=mesh['tmpl'=4,'row'=64] {'tmpl','row'}, use_global_device_ids=true, to_apply=%region_18.0 | all-reduce | flops 8704 | bytes 69632 | tf_op jit(solution)/shard_map/psum | solution.py:163
  377.6 162.2 %all-reduce.3.cloned.1.call-done = f32[2,64,320]{2,1,0:T(8,128)} async-done(((f32[2,64,320]{2,1,0:T(8,128)}), f32[2,64,320]{2,1,0:T(8,128)}) %all-reduce.3.cloned.1.call-update) | async-done | bytes 163856 | tf_op jit(solution)/shard_map/psum | solution.py:163
  (153 shorter events, 101.3 us)
Async XLA Ops:
  13.5 18.6 %copy-start.3 = (bf16[1,64,8,512]{3,2,1,0:T(8,128)(2,1)S(1)}, bf16[1,64,8,512]{3,2,1,0:T(8,128)(2,1)}, u32[]{:S(2)}) copy-start(bf16[1,64,8,512]{3,2,1,0:T(8,128)(2,1)} %param.12) | copy-start | bytes 1572868
  15.8 17.4 %copy-start.13 = (bf16[64,8,512]{2,0,1:T(8,128)(2,1)}, bf16[64,8,512]{2,0,1:T(8,128)(2,1)S(1)}, u32[]{:S(2)}) copy-start(bf16[64,8,512]{2,0,1:T(8,128)(2,1)S(1)} %get-tuple-element.42) | copy-start | bytes 1572868
  15.8 16.7 %copy-start.15 = (bf16[2,64,64]{2,1,0:T(8,128)(2,1)S(1)}, bf16[2,64,64]{2,1,0:T(8,128)(2,1)}, u32[]{:S(2)}) copy-start(bf16[2,64,64]{2,1,0:T(8,128)(2,1)} %param.15) | copy-start | bytes 49156
  16.9 30.9 %all-to-all-start = ((bf16[64,8,512]{2,1,0:T(8,128)(2,1)}), bf16[64,8,512]{2,1,0:T(8,128)(2,1)S(1)}, u32[]{:S(2)}, u32[]{:S(2)}) async-start(bf16[64,8,512]{2,1,0:T(8,128)(2,1)} %copy.45), calls=%async_computation | async-start | bytes 1048576 | tf_op jit(solution)/shard_map/all_to_all | solution.py:135
  47.9 23.0 %all-to-all-start.1 = ((bf16[64,8,512]{2,1,0:T(8,128)(2,1)}), bf16[64,8,512]{2,1,0:T(8,128)(2,1)S(1)}, u32[]{:S(2)}, u32[]{:S(2)}) async-start(bf16[64,8,512]{2,1,0:T(8,128)(2,1)} %copy.47), calls=%async_computation.1 | async-start | bytes 1048576 | tf_op jit(solution)/shard_map/all_to_all | solution.py:133
  70.9 23.9 %all-to-all-start.3 = ((bf16[64,8,512]{2,1,0:T(8,128)(2,1)}), bf16[64,8,512]{2,1,0:T(8,128)(2,1)}, u32[]{:S(2)}, u32[]{:S(2)}) async-start(bf16[64,8,512]{2,1,0:T(8,128)(2,1)} %copy.52), calls=%async_computation.3 | async-start | bytes 1048576 | tf_op jit(solution)/shard_map/all_to_all | solution.py:134
  81.0 23.5 %copy-start.2 = (bf16[1,64,8,512]{3,2,1,0:T(8,128)(2,1)S(1)}, bf16[1,64,8,512]{3,2,1,0:T(8,128)(2,1)}, u32[]{:S(2)}) copy-start(bf16[1,64,8,512]{3,2,1,0:T(8,128)(2,1)} %param.9) | copy-start | bytes 1572868
  81.0 23.6 %copy-start.5 = (bf16[1,64,8,512]{3,2,1,0:T(8,128)(2,1)S(1)}, bf16[1,64,8,512]{3,2,1,0:T(8,128)(2,1)}, u32[]{:S(2)}) copy-start(bf16[1,64,8,512]{3,2,1,0:T(8,128)(2,1)} %param.10) | copy-start | bytes 1572868
  94.8 24.0 %all-to-all-start.2 = ((bf16[64,2,2048]{2,1,0:T(2,128)(2,1)}), bf16[64,2,2048]{2,1,0:T(2,128)(2,1)}, u32[]{:S(2)}, u32[]{:S(2)}) async-start(bf16[64,2,2048]{2,1,0:T(2,128)(2,1)} %reshape.195), calls=%async_computation.2 | async-start | bytes 1048576 | tf_op jit(solution)/shard_map/all_to_all | solution.py:109
  107.1 21.9 %copy-start.14 = (bf16[2,64,320]{2,1,0:T(8,128)(2,1)S(1)}, bf16[2,64,320]{2,1,0:T(8,128)(2,1)}, u32[]{:S(2)}) copy-start(bf16[2,64,320]{2,1,0:T(8,128)(2,1)} %param.14) | copy-start | bytes 245764
  118.7 24.2 %all-to-all-start.4 = ((bf16[64,2,2048]{2,1,0:T(2,128)(2,1)}), bf16[64,2,2048]{2,1,0:T(2,128)(2,1)S(1)}, u32[]{:S(2)}, u32[]{:S(2)}) async-start(bf16[64,2,2048]{2,1,0:T(2,128)(2,1)} %reshape.197), calls=%async_computation.4 | async-start | bytes 1048576 | tf_op jit(solution)/shard_map/all_to_all | solution.py:110
  132.3 18.2 %slice-start.4 = ((s8[5242880]{0:T(1024)(128)(4,1)}), s8[1048576]{0:T(1024)(128)(4,1)S(1)}, s32[]{:S(2)}) async-start(s8[5242880]{0:T(1024)(128)(4,1)} %bitcast.374), calls=%async_computation.17 | async-start | bytes 2097152
  144.7 5.8 %slice-start.5 = ((s8[5242880]{0:T(1024)(128)(4,1)}), s8[4194304]{0:T(1024)(128)(4,1)S(1)}, s32[]{:S(2)}) async-start(s8[5242880]{0:T(1024)(128)(4,1)} %bitcast.374), calls=%async_computation.18 | async-start | bytes 8388608
  152.1 3.5 slice-start.1
  155.7 13.2 %copy-start.6 = (bf16[1,64,8,512]{3,2,1,0:T(8,128)(2,1)S(1)}, bf16[1,64,8,512]{3,2,1,0:T(8,128)(2,1)}, u32[]{:S(2)}) copy-start(bf16[1,64,8,512]{3,2,1,0:T(8,128)(2,1)} %param.10) | copy-start | bytes 1572868
  159.2 24.0 %all-to-all-start.6 = ((bf16[64,8,512]{2,1,0:T(8,128)(2,1)}), bf16[64,8,512]{2,1,0:T(8,128)(2,1)}, u32[]{:S(2)}, u32[]{:S(2)}) async-start(bf16[64,8,512]{2,1,0:T(8,128)(2,1)} %copy.61), calls=%async_computation.6 | async-start | bytes 1048576 | tf_op jit(solution)/shard_map/all_to_all | solution.py:152
  183.2 24.1 %all-to-all-start.5 = ((bf16[64,8,512]{2,1,0:T(8,128)(2,1)}), bf16[64,8,512]{2,1,0:T(8,128)(2,1)}, u32[]{:S(2)}, u32[]{:S(2)}) async-start(bf16[64,8,512]{2,1,0:T(8,128)(2,1)} %copy.60), calls=%async_computation.5 | async-start | bytes 1048576 | tf_op jit(solution)/shard_map/all_to_all | solution.py:150
  207.3 24.0 %all-to-all-start.8 = ((bf16[64,8,512]{2,1,0:T(8,128)(2,1)}), bf16[64,8,512]{2,1,0:T(8,128)(2,1)}, u32[]{:S(2)}, u32[]{:S(2)}) async-start(bf16[64,8,512]{2,1,0:T(8,128)(2,1)} %copy.66), calls=%async_computation.8 | async-start | bytes 1048576 | tf_op jit(solution)/shard_map/all_to_all | solution.py:151
  231.2 23.6 %all-to-all-start.7 = ((bf16[64,2,2048]{2,1,0:T(2,128)(2,1)}), bf16[64,2,2048]{2,1,0:T(2,128)(2,1)S(1)}, u32[]{:S(2)}, u32[]{:S(2)}) async-start(bf16[64,2,2048]{2,1,0:T(2,128)(2,1)} %reshape.199), calls=%async_computation.7 | async-start | bytes 1048576 | tf_op jit(solution)/shard_map/all_to_all | solution.py:109
  254.9 23.5 %all-to-all-start.9 = ((bf16[64,2,2048]{2,1,0:T(2,128)(2,1)}), bf16[64,2,2048]{2,1,0:T(2,128)(2,1)}, u32[]{:S(2)}, u32[]{:S(2)}) async-start(bf16[64,2,2048]{2,1,0:T(2,128)(2,1)} %reshape.201), calls=%async_computation.9 | async-start | bytes 1048576 | tf_op jit(solution)/shard_map/all_to_all | solution.py:110
  264.5 275.2 %all-reduce.3.cloned.1.call-start = ((), (), s32[]{:S(2)}) async-start(), calls=%async_computation.11 | async-start | bytes 393216 | tf_op jit(solution)/shard_map/psum | solution.py:163
  269.0 19.6 %slice-start.2 = ((s8[5242880]{0:T(1024)(128)(4,1)}), s8[1048576]{0:T(1024)(128)(4,1)S(1)}, s32[]{:S(2)}) async-start(s8[5242880]{0:T(1024)(128)(4,1)} %bitcast.372), calls=%async_computation.15 | async-start | bytes 2097152
  282.8 5.8 %slice-start.3 = ((s8[5242880]{0:T(1024)(128)(4,1)}), s8[4194304]{0:T(1024)(128)(4,1)S(1)}, s32[]{:S(2)}) async-start(s8[5242880]{0:T(1024)(128)(4,1)} %bitcast.372), calls=%async_computation.16 | async-start | bytes 8388608
  293.5 247.9 %reduce-scatter.4.cloned.1.call-start = ((), (), s32[]{:S(2)}) async-start(), calls=%async_computation.12 | async-start | bytes 655360
  (11 other events, 18.7 us)
Sparse Core Ops, SparseCore 0:
  293.6 246.0 all-reduce.2
Sparse Core Ops, SparseCore 1:
  296.5 21.0 reduce-scatter.3
where the time goes:
time: 559 us; the launch traced here: 551 us
  waiting for transfers between devices  242 us (43%)
  starting transfers between devices  101 us (18%)
  blocking collectives  79.3 us (14%)
  other arithmetic  50.3 us (9%)
  local copies, waits for them, and re-layouts  37.8 us (7%)
  matrix products  24.1 us (4%)
  between operations  16.5 us (3%)
    psum x1, waiting for transfers between devices, shards(): summed = lax.psum(stacked, ('tmpl', 'row'))  162 us
    psum x1, blocking collectives, shards(): summed = lax.psum(stacked, ('tmpl', 'row'))  79.3 us
    unnamed x15, other arithmetic  27.8 us
    unnamed x59, local copies, waits for them, and re-layouts  26.1 us
    all_to_all x2, starting transfers between devices, send_back(): lax.all_to_all(grad_b, 'row', split_axis=1, concat_axis=0, tiled=True)  19.4 us
    all_to_all x2, starting transfers between devices, send_back(): lax.all_to_all(grad_a, 'row', split_axis=1, concat_axis=0, tiled=True)  19.3 us
    all_to_all x1, starting transfers between devices, shards(): lax.all_to_all(state_in[5], 'row', split_axis=0, concat_axis=1, tiled=True)  15.1 us
    all_to_all x1, waiting for transfers between devices, shards(): lax.all_to_all(head_in[0], 'row', split_axis=0, concat_axis=1, tiled=True)  13.6 us
  transfers between devices with their start and end apart: 12, of which 11 were waited for; matrix products, arithmetic and copies ran while one was open for 13% of the time, Pallas kernels for 0%

commit v1 on v0

v1 whole, which is shorter than its diff:
```python
import functools

import jax
import jax.numpy as jnp
from jax import lax
from jax.experimental import pallas as pl
from jax.experimental.pallas import tpu as pltpu
from jax.sharding import PartitionSpec as P

EPSILON = 1e-05
F32 = jnp.float32
BF16 = jnp.bfloat16
MESH = pl.DeviceIdType.MESH
CH = 64
RB = 8
COLS = 512
ROWS = 512
PEERS = 64
HALF = 16


def sigmoid(values):
    return 0.5 * jnp.tanh(0.5 * values) + 0.5


def product(left, right, dims=((1,), (0,))):
    return lax.dot_general(left, right, (dims, ((), ())), preferred_element_type=F32)


def kernel(
    saved_out, sum_out, saved_in, sum_in, cotangent, w_in, w_out, gain, shift,
    trunk, params,
    weights_p, weights_q, weights_u, weights_d, perm,
    normed, normed_sum, gated, proj, stat, work, upstream, d_proj, mats, partial,
    lanes_l, lanes_r,
    send_ab, recv_ab, send_d, recv_d, send_g, recv_g, send_r, recv_r,
    param, recv_one, sum_one, recv_two, recv_three,
    send_sem, recv_sem,
):
    tm = lax.axis_index("tmpl")
    me = lax.axis_index("row")
    saved = (saved_out, saved_in)
    sums = (sum_out, sum_in)

    barrier = pltpu.get_barrier_semaphore()

    def greet_row(step, carry):
        pl.semaphore_signal(
            barrier, inc=1, device_id={"tmpl": tm, "row": me ^ step}, device_id_type=MESH
        )
        return carry

    lax.fori_loop(1, PEERS, greet_row, 0)

    def greet_tmpl(step, carry):
        pl.semaphore_signal(
            barrier, inc=1,
            device_id={"tmpl": tm ^ (step // 4), "row": me ^ (step % 4)}, device_id_type=MESH,
        )
        return carry

    lax.fori_loop(4, 16, greet_tmpl, 0)

    def expand_rows(table, dest, count, width, start):
        lane = lax.broadcasted_iota(jnp.int32, (RB, width), 1)
        row = lax.broadcasted_iota(jnp.int32, (RB, width), 0)
        mask = jnp.where((lane & 7) == row, 1.0, 0.0).astype(F32)

        def body(step, carry):
            block = work[pl.ds(pl.multiple_of(8 * step, 8), 8), :width]
            parts = [block[k : k + 1, :] * mask for k in range(8)]
            at = pl.multiple_of(64 * step, 64)
            dest[pl.ds(at, 64), start : start + width] = jnp.concatenate(parts, 0).astype(BF16)
            return carry

        lax.fori_loop(0, count // 8, body, 0)

    def one_hot(rows):
        width = rows * 8
        lane = lax.broadcasted_iota(jnp.int32, (rows, width), 1)
        row = lax.broadcasted_iota(jnp.int32, (rows, width), 0)
        return jnp.where((lane >> 3) == row, 1.0, 0.0).astype(BF16)

    def build_forward(d):
        spread = one_hot(CH)
        work[0:320, :] = product(w_in[d], spread, ((0,), (0,)))
        expand_rows(None, weights_p, 320, COLS, 0)

    def build_backward(d):
        spread = one_hot(CH)
        for part in range(5):
            work[0:CH, :] = product(w_in[d, :, part * CH : (part + 1) * CH], spread)
            expand_rows(None, weights_q, CH, COLS, part * COLS)

    def build_output(d):
        spread = one_hot(CH)
        work[0:CH, :] = product(w_out[d], spread, ((0,), (0,)))
        expand_rows(None, weights_u, CH, COLS, 0)
        work[0:CH, :] = product(w_out[d], spread)
        expand_rows(None, weights_d, CH, COLS, 0)

    def statistics(x_ref, slot):
        zero = jnp.zeros((RB, COLS), F32)

        def add(step, acc):
            for k in range(4):
                acc = acc + x_ref[4 * step + k].astype(F32)
            return acc

        mean = lax.fori_loop(0, CH // 4, add, zero) * (1.0 / CH)

        def square(step, acc):
            for k in range(4):
                off = x_ref[4 * step + k].astype(F32) - mean
                acc = acc + off * off
            return acc

        inv = lax.rsqrt(lax.fori_loop(0, CH // 4, square, zero) * (1.0 / CH) + EPSILON)
        stat[slot, 0] = mean
        stat[slot, 1] = inv
        return mean, inv

    def normalise(x_ref, mean, inv, slot, dest):
        def body(step, carry):
            parts = []
            for k in range(4):
                c = 4 * step + k
                standard = (x_ref[c].astype(F32) - mean) * inv
                parts.append(standard * gain[slot, c] + shift[slot, c])
            at = pl.multiple_of(32 * step, 32)
            dest[pl.ds(at, 32), :] = jnp.concatenate(parts, 0).astype(BF16)
            return carry

        lax.fori_loop(0, CH // 4, body, 0)

    def prepare(d):
        mean, inv = statistics(saved[d], 2 * d)
        normalise(saved[d], mean, inv, 2 * d, normed.at[d])

        def project(step, carry):
            at = pl.multiple_of(step * ROWS, ROWS)
            proj[d, step] = product(weights_p[pl.ds(at, ROWS), :], normed[d])
            return carry

        lax.fori_loop(0, 5, project, 0)

        def pairs(step, carry):
            rows = pl.ds(pl.multiple_of(16 * step, 16), 16)
            chans = pl.ds(2 * step, 2)
            for k in range(2):
                gate = sigmoid(proj[d, 2 * k, rows, :])
                proj[d, 2 * k, rows, :] = gate
                pair = gate * proj[d, 2 * k + 1, rows, :]
                send_ab[d, chans, k] = pair.reshape(2, RB, COLS).astype(BF16)
            proj[d, 4, rows, :] = sigmoid(proj[d, 4, rows, :])
            return carry

        lax.fori_loop(0, CH // 2, pairs, 0)

    def head_first(d):
        mean, inv = statistics(sums[d], 2 * d + 1)
        normalise(sums[d], mean, inv, 2 * d + 1, normed_sum)

    def backward_sums(x_ref, mean, inv, slot):
        zero = jnp.zeros((RB, COLS), F32)

        def fold(v):
            return v[:, 0:128] + v[:, 128:256] + v[:, 256:384] + v[:, 384:512]

        def body(step, carry):
            one, two = carry
            for k in range(4):
                c = 4 * step + k
                dn = work[pl.ds(pl.multiple_of(8 * c, 8), 8), :]
                standard = (x_ref[c].astype(F32) - mean) * inv
                scaled = dn * gain[slot, c]
                one = one + scaled
                two = two + scaled * standard
                partial[0, c] = fold(dn * standard)
                partial[1, c] = fold(dn)
            return one, two

        one, two = lax.fori_loop(0, CH // 4, body, (zero, zero))
        return one * (1.0 / CH), two * (1.0 / CH)

    def small_sums(d, k):
        lane = lax.broadcasted_iota(jnp.int32, (CH, 128), 1)
        total = jnp.zeros((CH, 128), F32)
        for j in range(2):
            column = jnp.sum(jnp.sum(partial[j], axis=1), axis=1, keepdims=True)
            total = total + jnp.where(lane == 2 * j + k, column, 0.0)
        return total

    def store_params(d, start, value, width):
        for block in range(8):
            for lo in range(0, width, 128):
                size = min(128, width - lo)
                at = start + lo
                half, lane = at // 256, at % 256
                param[block * 2 + half, d, :, lane : lane + size] = (
                    value[block * 8 : block * 8 + 8, lo : lo + size]
                )

    def head_second(d, read_up):
        def gating(step, carry):
            rows = pl.ds(pl.multiple_of(16 * step, 16), 16)
            gated[rows, :] = (proj[d, 4, rows, :] * read_up(step)).astype(BF16)
            return carry

        lax.fori_loop(0, CH // 2, gating, 0)
        work[...] = product(weights_u[...], normed_sum[...])

        def last_block(step, carry):
            rows = pl.ds(pl.multiple_of(16 * step, 16), 16)
            gate = proj[d, 4, rows, :]
            d_gate = read_up(step) * work[rows, :]
            at = pl.ds(pl.multiple_of(4 * ROWS + 16 * step, 16), 16)
            d_proj[at, :] = (d_gate * gate * (1.0 - gate)).astype(BF16)
            return carry

        lax.fori_loop(0, CH // 2, last_block, 0)
        work[...] = product(weights_d[...], gated[...])
        slot = 2 * d + 1
        mean, inv = stat[slot, 0], stat[slot, 1]
        one, two = backward_sums(sums[d], mean, inv, slot)

        def finish(step, carry):
            for k in range(4):
                c = 4 * step + k
                dn = work[pl.ds(pl.multiple_of(8 * c, 8), 8), :]
                standard = (sums[d][c].astype(F32) - mean) * inv
                send_d[d, c] = (inv * (dn * gain[slot, c] - one - standard * two)).astype(BF16)
            return carry

        lax.fori_loop(0, CH // 4, finish, 0)

    def spread_lanes(source, dest, start):
        moved = product(perm[...], source).astype(BF16)
        for r in range(RB):
            dest[start : start + CH, r * COLS : (r + 1) * COLS] = moved[r * CH : (r + 1) * CH, :]

    def head_params(d):
        spread_lanes(normed_sum[...], lanes_l, 0)
        spread_lanes(gated[...], lanes_r, 0)
        store_params(d, 320, product(lanes_l[...], lanes_r[0:CH, :], ((1,), (1,))), CH)
        small = small_sums(d, 1)
        store_params(d, 384, small, 128)

    def tail(d, emit):
        def blocks(step, carry):
            rows = pl.ds(pl.multiple_of(16 * step, 16), 16)
            chans = pl.ds(2 * step, 2)
            for k in range(2):
                grad = recv_g[d, chans, k].astype(F32).reshape(16, COLS)
                gate = proj[d, 2 * k, rows, :]
                value = proj[d, 2 * k + 1, rows, :]
                at = pl.ds(pl.multiple_of(2 * k * ROWS + 16 * step, 16), 16)
                d_proj[at, :] = (grad * value * gate * (1.0 - gate)).astype(BF16)
                at = pl.ds(pl.multiple_of((2 * k + 1) * ROWS + 16 * step, 16), 16)
                d_proj[at, :] = (grad * gate).astype(BF16)
            return carry

        lax.fori_loop(0, CH // 2, blocks, 0)
        work[...] = product(weights_q[...], d_proj[...])
        slot = 2 * d
        mean, inv = stat[slot, 0], stat[slot, 1]
        one, two = backward_sums(saved[d], mean, inv, slot)

        def finish(step, carry):
            for k in range(4):
                c = 4 * step + k
                rows = pl.ds(pl.multiple_of(8 * c, 8), 8)
                dn = work[rows, :]
                standard = (saved[d][c].astype(F32) - mean) * inv
                emit(c, rows, inv * (dn * gain[slot, c] - one - standard * two))
            return carry

        lax.fori_loop(0, CH // 4, finish, 0)

    def tail_params(d):
        spread_lanes(normed[d], lanes_l, 0)
        for part in range(5):
            spread_lanes(d_proj[part * ROWS : (part + 1) * ROWS, :], lanes_r, part * CH)
        store_params(d, 0, product(lanes_l[...], lanes_r[...], ((1,), (1,))), 320)
        small = small_sums(d, 0)
        for block in range(8):
            param[block * 2 + 1, d, :, 128:256] += small[block * 8 : block * 8 + 8, :]

    def exchange(source, dest, sem):
        def send(step, carry):
            peer = me ^ step
            pltpu.make_async_remote_copy(
                src_ref=source.at[peer], dst_ref=dest.at[me],
                send_sem=send_sem.at[sem], recv_sem=recv_sem.at[sem],
                device_id={"tmpl": tm, "row": peer}, device_id_type=MESH,
            ).start()
            return carry

        lax.fori_loop(1, PEERS, send, 0)
        dest[me] = source[me]

    def wait_recv(dest, sem, count):
        view = dest.at[pl.ds(0, count)]
        pltpu.make_async_copy(view, view, recv_sem.at[sem]).wait()

    def wait_send(source, sem, count):
        view = source.at[pl.ds(0, count)]
        pltpu.make_async_copy(view, view, send_sem.at[sem]).wait()

    def triangle(d):
        def load(step, carry):
            rows = pl.ds(pl.multiple_of(16 * step, 16), 16)
            peers = pl.ds(2 * step, 2)
            mats[0, rows, :] = recv_ab[d, peers, 0].astype(F32).reshape(16, COLS).astype(BF16)
            mats[1, rows, :] = recv_ab[d, peers, 1].astype(F32).reshape(16, COLS).astype(BF16)
            mats[2, rows, :] = recv_d[d, peers].astype(F32).reshape(16, COLS).astype(BF16)
            return carry

        lax.fori_loop(0, PEERS // 2, load, 0)

        def store(k):
            def body(step, carry):
                rows = pl.ds(pl.multiple_of(16 * step, 16), 16)
                send_g[d, pl.ds(2 * step, 2), k] = work[rows, :].reshape(2, RB, COLS).astype(BF16)
                return carry

            lax.fori_loop(0, PEERS // 2, body, 0)

        if d == 0:
            work[...] = product(mats[2], mats[1])
            store(0)
            work[...] = product(mats[2], mats[0], ((0,), (0,)))
            store(1)
        else:
            work[...] = product(mats[1], mats[2], ((1,), (1,)))
            store(0)
            work[...] = product(mats[0], mats[2])
            store(1)

    def read_cotangent(step):
        return cotangent[pl.ds(2 * step, 2)].astype(F32).reshape(16, COLS)

    def read_upstream(step):
        return upstream[pl.ds(pl.multiple_of(16 * step, 16), 16), :]

    build_forward(1)
    prepare(1)
    pl.semaphore_wait(barrier, PEERS - 1 + 12)
    exchange(send_ab.at[1], recv_ab.at[1], 0)
    build_output(1)
    head_first(1)
    head_second(1, read_cotangent)
    exchange(send_d.at[1], recv_d.at[1], 1)

    build_forward(0)
    prepare(0)
    exchange(send_ab.at[0], recv_ab.at[0], 3)
    lane = lax.broadcasted_iota(jnp.int32, (ROWS, ROWS), 1)
    row = lax.broadcasted_iota(jnp.int32, (ROWS, ROWS), 0)
    perm[...] = jnp.where(lane == ((row & 63) << 3) + (row >> 6), 1.0, 0.0).astype(BF16)
    head_params(1)
    build_backward(1)

    wait_recv(recv_ab.at[1], 0, PEERS - 1)
    wait_recv(recv_d.at[1], 1, PEERS - 1)
    triangle(1)
    exchange(send_g.at[1], recv_g.at[1], 2)
    build_output(0)
    head_first(0)

    wait_recv(recv_g.at[1], 2, PEERS - 1)

    def keep(c, rows, value):
        upstream[rows, :] = cotangent[c].astype(F32) + value

    tail(1, keep)
    tail_params(1)
    head_second(0, read_upstream)
    exchange(send_d.at[0], recv_d.at[0], 4)
    head_params(0)
    build_backward(0)

    wait_recv(recv_ab.at[0], 3, PEERS - 1)
    wait_recv(recv_d.at[0], 4, PEERS - 1)
    triangle(0)
    exchange(send_g.at[0], recv_g.at[0], 5)
    wait_recv(recv_g.at[0], 5, PEERS - 1)

    def spread(c, rows, value):
        total = (upstream[rows, :] + value).astype(BF16)
        for t in range(4):
            send_r[t, c] = total[:, t * 128 : (t + 1) * 128]

    tail(0, spread)

    def send_trunk(step, carry):
        peer = tm ^ step
        pltpu.make_async_remote_copy(
            src_ref=send_r.at[peer], dst_ref=recv_r.at[tm],
            send_sem=send_sem.at[6], recv_sem=recv_sem.at[6],
            device_id={"tmpl": peer, "row": me}, device_id_type=MESH,
        ).start()
        return carry

    lax.fori_loop(1, 4, send_trunk, 0)
    recv_r[tm] = send_r[tm]
    tail_params(0)

    deep, flat = me // 4, me % 4

    def send_one(step, carry):
        peer = deep ^ step
        pltpu.make_async_remote_copy(
            src_ref=param.at[peer], dst_ref=recv_one.at[deep],
            send_sem=send_sem.at[7], recv_sem=recv_sem.at[7],
            device_id={"tmpl": tm, "row": peer * 4 + flat}, device_id_type=MESH,
        ).start()
        return carry

    lax.fori_loop(1, HALF, send_one, 0)
    recv_one[deep] = param[deep]
    wait_recv(recv_one, 7, HALF - 1)
    total = recv_one[0]
    for k in range(1, HALF):
        total = total + recv_one[k]
    sum_one[0] = total
    place = tm * 4 + flat

    def send_two(step, carry):
        pltpu.make_async_remote_copy(
            src_ref=sum_one.at[0], dst_ref=recv_two.at[place],
            send_sem=send_sem.at[8], recv_sem=recv_sem.at[8],
            device_id={"tmpl": tm ^ (step // 4), "row": deep * 4 + (flat ^ (step % 4))},
            device_id_type=MESH,
        ).start()
        return carry

    lax.fori_loop(1, HALF, send_two, 0)
    recv_two[place] = sum_one[0]
    wait_recv(recv_two, 8, HALF - 1)
    total = recv_two[0]
    for k in range(1, HALF):
        total = total + recv_two[k]
    sum_one[1] = total * (1.0 / 2048.0)

    def send_three(step, carry):
        pltpu.make_async_remote_copy(
            src_ref=sum_one.at[1], dst_ref=recv_three.at[deep],
            send_sem=send_sem.at[9], recv_sem=recv_sem.at[9],
            device_id={"tmpl": tm, "row": (deep ^ step) * 4 + flat}, device_id_type=MESH,
        ).start()
        return carry

    lax.fori_loop(1, HALF, send_three, 0)
    recv_three[deep] = sum_one[1]

    wait_recv(recv_r, 6, 3)

    def gather_trunk(step, carry):
        chans = pl.ds(4 * step, 4)
        value = recv_r[0, chans].astype(F32)
        for t in range(1, 4):
            value = value + recv_r[t, chans].astype(F32)
        trunk[chans] = value.astype(BF16)
        return carry

    lax.fori_loop(0, CH // 4, gather_trunk, 0)

    wait_recv(recv_three, 9, HALF - 1)
    for block in range(8):
        for half in range(2):
            for d in range(2):
                params[d, block * 8 : block * 8 + 8, half * 256 : half * 256 + 256] = (
                    recv_three[block * 2 + half, d]
                )
    for d, base in ((1, 0), (0, 3)):
        wait_send(send_ab.at[d], base, PEERS - 1)
        wait_send(send_d.at[d], base + 1, PEERS - 1)
        wait_send(send_g.at[d], base + 2, PEERS - 1)
    wait_send(send_r, 6, 3)
    wait_send(param, 7, HALF - 1)
    wait_send(recv_two, 8, HALF - 1)
    wait_send(recv_three, 9, HALF - 1)


def shards(saved_out, sum_out, saved_in, sum_in, cotangent, w_in, w_out, norm_gain, norm_shift):
    vmem = pl.BlockSpec(memory_space=pltpu.VMEM)
    smem = pl.BlockSpec(memory_space=pltpu.SMEM)
    flat = 2 * 2
    trunk, params = pl.pallas_call(
        kernel,
        out_shape=(
            jax.ShapeDtypeStruct((CH, RB, 128), BF16),
            jax.ShapeDtypeStruct((2, CH, 512), F32),
        ),
        in_specs=[vmem] * 7 + [smem] * 2,
        out_specs=(vmem, vmem),
        scratch_shapes=[
            pltpu.VMEM((5 * ROWS, COLS), BF16),
            pltpu.VMEM((ROWS, 5 * COLS), BF16),
            pltpu.VMEM((ROWS, COLS), BF16),
            pltpu.VMEM((ROWS, COLS), BF16),
            pltpu.VMEM((ROWS, ROWS), BF16),
            pltpu.VMEM((2, ROWS, COLS), BF16),
            pltpu.VMEM((ROWS, COLS), BF16),
            pltpu.VMEM((ROWS, COLS), BF16),
            pltpu.VMEM((2, 5, ROWS, COLS), F32),
            pltpu.VMEM((4, 2, RB, COLS), F32),
            pltpu.VMEM((ROWS, COLS), F32),
            pltpu.VMEM((ROWS, COLS), F32),
            pltpu.VMEM((5 * ROWS, COLS), BF16),
            pltpu.VMEM((3, ROWS, COLS), BF16),
            pltpu.VMEM((2, CH, RB, 128), F32),
            pltpu.VMEM((CH, RB * COLS), BF16),
            pltpu.VMEM((5 * CH, RB * COLS), BF16),
            pltpu.VMEM((2, PEERS, 2, RB, COLS), BF16),
            pltpu.VMEM((2, PEERS, 2, RB, COLS), BF16),
            pltpu.VMEM((2, PEERS, RB, COLS), BF16),
            pltpu.VMEM((2, PEERS, RB, COLS), BF16),
            pltpu.VMEM((2, PEERS, 2, RB, COLS), BF16),
            pltpu.VMEM((2, PEERS, 2, RB, COLS), BF16),
            pltpu.VMEM((4, CH, RB, 128), BF16),
            pltpu.VMEM((4, CH, RB, 128), BF16),
            pltpu.VMEM((HALF, 2, 8, 256), F32),
            pltpu.VMEM((HALF, 2, 8, 256), F32),
            pltpu.VMEM((2, 2, 8, 256), F32),
            pltpu.VMEM((HALF, 2, 8, 256), F32),
            pltpu.VMEM((HALF, 2, 8, 256), F32),
            pltpu.SemaphoreType.DMA((10,)),
            pltpu.SemaphoreType.DMA((10,)),
        ],
        compiler_params=pltpu.CompilerParams(
            collective_id=0, has_side_effects=True, vmem_limit_bytes=58 * 1024 * 1024
        ),
        name="triangle_backward",
    )(
        saved_out[0], sum_out[0], saved_in[0], sum_in[0], cotangent[0], w_in, w_out,
        norm_gain.reshape(flat, CH), norm_shift.reshape(flat, CH),
    )
    small = params[:, :, 384:388].transpose(0, 2, 1)
    return trunk, params[:, :, :320], params[:, :, 320:384], small[:, 0:2], small[:, 2:4]


def solution(mesh):
    whole = P("tmpl", None, "row", None)
    in_specs = (whole, whole, whole, whole, whole, P(), P(), P(), P())
    out_specs = (P(None, "row", "tmpl"), P(), P(), P(), P())
    return jax.shard_map(shards, mesh=mesh, in_specs=in_specs, out_specs=out_specs, check_vma=False)
```

time: 559 us -> 189 us (0.34); the launches traced: 551 us -> 189 us
  waiting for transfers between devices: 242 us -> 0 us
  Pallas kernels: 0 us -> 184 us
  starting transfers between devices: 101 us -> 0 us
  blocking collectives: 79.3 us -> 0 us
  other arithmetic: 50.3 us -> 0 us
  local copies, waits for them, and re-layouts: 37.8 us -> 4.57 us
  matrix products: 24.1 us -> 0 us
  between operations: 16.5 us -> 0.66 us
    pallas_call x0 -> x1, Pallas kernels: none -> 184 us  [shards(): pl.pallas_call(kernel, out_shape=(jax.ShapeDtypeStruct((CH, RB, 128), BF1...]
    psum x1 -> x0, waiting for transfers between devices: 162 us -> none  [shards(): summed = lax.psum(stacked, ('tmpl', 'row'))]
    all_to_all x10 -> x0, starting transfers between devices: 101 us -> none  [the longest x2 19.4 us: send_back(): lax.all_to_all(grad_b, 'row', split_axis=1, concat_axis=0, tiled=True)]
    all_to_all x10 -> x0, waiting for transfers between devices: 79.6 us -> none  [the longest x1 13.6 us: shards(): lax.all_to_all(head_in[0], 'row', split_axis=0, concat_axis=1, tiled=True)]
    psum x1 -> x0, blocking collectives: 79.3 us -> none  [shards(): summed = lax.psum(stacked, ('tmpl', 'row'))]
    unnamed x15 -> x0, other arithmetic: 27.8 us -> none
    dot_general x16 -> x0, matrix products: 24.1 us -> none  [the longest x2 5.43 us: prepare(): jnp.einsum('cf,crn->frn', weight_in, normed_b, preferred_element_type=jnp...]
    unnamed x59 -> x7, local copies, waits for them, and re-layouts: 26.1 us -> 2.17 us
  transfers between devices with their start and end apart: 12 -> 0, of which waited for: 11 -> 0; matrix products, arithmetic and copies ran while one was open for 13% -> 0% of each run, Pallas kernels for 0% -> 0%
where the time goes in v1:
time: 189 us
  Pallas kernels  184 us (97%)
  local copies, waits for them, and re-layouts  4.57 us (2%)
    pallas_call x1, Pallas kernels, shards(): pl.pallas_call(kernel, out_shape=(jax.ShapeDtypeStruct((CH, RB, 128), BF1...  184 us

profile of v1, /device:TPU:1, one launch (start us, length us, event | category | flops | bytes accessed | tf_op | source)
XLA Modules:
  0.0 188.9 jit_solution(17203160141075801810)
XLA Ops:
  0.6 183.7 %triangle_backward.1 = (bf16[64,8,128]{2,1,0:T(8,128)(2,1)}, f32[2,64,512]{2,1,0:T(8,128)}) custom-call(bf16[64,8,512]{2,1,0:T(8,128)(2,1)} %bitcast.9, bf16[64,8,512]{2,1,0:T(8,128)(2,1)} %bitcast.10, bf16[64,8,512]{2,1,0:T(8,128)(2,1)} %bitcast.11, bf16[64,8,512]{2,1,0:T(8,128)(2,1)} %bitcast.12, bf16[64,8,512]{2,1,0:T(8,128)(2,1)} %bitcast.13, ...), custom_call_target="tpu_custom_call" | custom-call | tf_op jit(solution)/shard_map/triangle_backward/pallas_call | solution.py:490
  184.3 0.0 copy-start
  184.3 0.9 slice_bitcast_fusion
  185.2 0.1 fusion
  185.3 0.7 copy.14
  186.0 0.7 copy.15
  186.6 0.0 copy-done
  186.6 0.7 slice.15
  187.3 0.0 copy-start.1
  187.3 0.7 slice.16
  188.0 0.2 copy-done.1
  188.2 0.7 copy.17
Async XLA Ops:
  184.3 2.3 %copy-start = (f32[2,64,512]{2,1,0:T(8,128)S(1)}, f32[2,64,512]{2,1,0:T(8,128)}, u32[]{:S(2)}) copy-start(f32[2,64,512]{2,1,0:T(8,128)} %get-tuple-element.8) | copy-start | bytes 786436
  187.3 0.9 copy-start.1

commit v2 on v0

v2 whole, which is shorter than its diff:
```python
import functools

import jax
import jax.numpy as jnp
from jax import lax
from jax.experimental import pallas as pl
from jax.experimental.pallas import tpu as pltpu
from jax.sharding import PartitionSpec as P

EPSILON = 1e-05
F32 = jnp.float32
BF16 = jnp.bfloat16
MESH = pl.DeviceIdType.MESH
CH = 64
RB = 8
COLS = 512
ROWS = 512
PEERS = 64
HALF = 16


def sigmoid(values):
    return 0.5 * jnp.tanh(0.5 * values) + 0.5


def product(left, right, dims=((1,), (0,))):
    return lax.dot_general(left, right, (dims, ((), ())), preferred_element_type=F32)


def kernel(
    saved_out, sum_out, saved_in, sum_in, cotangent, w_in, w_out, gain, shift,
    trunk, totals,
    weights_p, weights_q, weights_u, weights_d, perm,
    normed, normed_sum, gated, proj, stat, work, update, upstream, grad_n, d_proj, mats, partial,
    lanes_n, lanes_s, lanes_r, small,
    outbox, inbox, result, send_r, recv_r, send_h, recv_h,
    param, recv_one, part_sum, recv_two,
    send_sem, recv_sem,
):
    tm = lax.axis_index("tmpl")
    me = lax.axis_index("row")
    deep, flat = me // 8, me % 8
    board, core = tm // 2, tm % 2
    saved = (saved_out, saved_in)
    sums = (sum_out, sum_in)

    barrier = pltpu.get_barrier_semaphore()

    def greet(tmpl, row):
        pl.semaphore_signal(
            barrier, inc=1, device_id={"tmpl": tmpl, "row": row}, device_id_type=MESH
        )

    def greet_row(step, carry):
        greet(tm, me ^ step)
        return carry

    lax.fori_loop(1, PEERS, greet_row, 0)

    def greet_rest(step, carry):
        greet(tm ^ 1, (deep ^ step) * 8 + flat)
        greet(tm ^ 2, deep * 8 + (flat ^ step))
        return carry

    lax.fori_loop(0, 8, greet_rest, 0)

    def rows_of(quad):
        return pl.ds(pl.multiple_of(32 * quad, 32), 32)

    def block_rows(block, quad):
        return pl.ds(pl.multiple_of(block * ROWS + 32 * quad, 32), 32)

    def to_rows(values):
        return values.astype(F32).reshape(4 * RB, COLS)

    def to_chans(values):
        return values.reshape(4, RB, COLS).astype(BF16)

    def expand_rows(table, dest, top, start):
        lane = lax.broadcasted_iota(jnp.int32, (RB, COLS), 1)
        row = lax.broadcasted_iota(jnp.int32, (RB, COLS), 0)
        mask = jnp.where((lane & 7) == row, 1.0, 0.0).astype(F32)
        work[0:CH, :] = table

        def body(step, carry):
            block = work[pl.ds(pl.multiple_of(8 * step, 8), 8), :]
            parts = [block[k : k + 1, :] * mask for k in range(8)]
            at = pl.multiple_of(top + 64 * step, 64)
            dest[pl.ds(at, 64), start : start + COLS] = jnp.concatenate(parts, 0).astype(BF16)
            return carry

        lax.fori_loop(0, CH // 8, body, 0)

    def one_hot():
        lane = lax.broadcasted_iota(jnp.int32, (CH, COLS), 1)
        row = lax.broadcasted_iota(jnp.int32, (CH, COLS), 0)
        return jnp.where((lane >> 3) == row, 1.0, 0.0).astype(BF16)

    def build_forward(d, blocks):
        spread = one_hot()
        for b in blocks:
            table = product(w_in[d, :, b * CH : (b + 1) * CH], spread, ((0,), (0,)))
            expand_rows(table, weights_p, b * ROWS, 0)

    def build_backward(d):
        spread = one_hot()
        for b in range(5):
            table = product(w_in[d, :, b * CH : (b + 1) * CH], spread)
            expand_rows(table, weights_q, 0, b * COLS)

    def build_output(d):
        spread = one_hot()
        expand_rows(product(w_out[d], spread, ((0,), (0,))), weights_u, 0, 0)
        expand_rows(product(w_out[d], spread), weights_d, 0, 0)

    def statistics(x_ref, slot):
        zero = jnp.zeros((RB, COLS), F32)

        def add(step, acc):
            for k in range(8):
                acc = acc + x_ref[8 * step + k].astype(F32)
            return acc

        mean = lax.fori_loop(0, CH // 8, add, zero) * (1.0 / CH)

        def square(step, acc):
            for k in range(8):
                off = x_ref[8 * step + k].astype(F32) - mean
                acc = acc + off * off
            return acc

        inv = lax.rsqrt(lax.fori_loop(0, CH // 8, square, zero) * (1.0 / CH) + EPSILON)
        stat[slot, 0] = mean
        stat[slot, 1] = inv
        return mean, inv

    def normalise(x_ref, mean, inv, slot, dest):
        def body(quad, carry):
            parts = []
            for k in range(4):
                c = 4 * quad + k
                standard = (x_ref[c].astype(F32) - mean) * inv
                parts.append(standard * gain[slot, c] + shift[slot, c])
            dest[rows_of(quad), :] = jnp.concatenate(parts, 0).astype(BF16)
            return carry

        lax.fori_loop(0, CH // 4, body, 0)

    def post(kind, peer):
        pltpu.make_async_remote_copy(
            src_ref=outbox.at[kind, peer], dst_ref=inbox.at[kind, me],
            send_sem=send_sem.at[kind], recv_sem=recv_sem.at[kind],
            device_id={"tmpl": tm, "row": peer}, device_id_type=MESH,
        ).start()

    def exchange(kind, fill):
        own = me // 4
        if fill is not None:
            fill(own)
        for k in range(1, 4):
            post(kind, me ^ k)

        def body(step, carry):
            quad = own ^ step
            if fill is not None:
                fill(quad)
            for k in range(4):
                post(kind, 4 * quad + k)
            return carry

        lax.fori_loop(1, PEERS // 4, body, 0)
        inbox[kind, me] = outbox[kind, me]

    def all_quads(fill):
        def body(quad, carry):
            fill(quad)
            return carry

        lax.fori_loop(0, PEERS // 4, body, 0)

    def wait_recv(dest, sem, count):
        view = dest.at[pl.ds(0, count)]
        pltpu.make_async_copy(view, view, recv_sem.at[sem]).wait()

    def wait_send(dest, sem, count):
        view = dest.at[pl.ds(0, count)]
        pltpu.make_async_copy(view, view, send_sem.at[sem]).wait()

    def arrived(kind):
        wait_recv(inbox.at[kind], kind, PEERS - 1)

    def sent(kind):
        wait_send(inbox.at[kind], kind, PEERS - 1)

    def project(d, blocks):
        for b in blocks:
            proj[d, b] = product(weights_p[b * ROWS : (b + 1) * ROWS, :], normed[d])

    def norm_input(d):
        mean, inv = statistics(saved[d], 2 * d)
        normalise(saved[d], mean, inv, 2 * d, normed.at[d])

    def pair_fill(d, k, kind):
        def fill(quad):
            rows = rows_of(quad)
            gate = sigmoid(proj[d, 2 * k, rows, :])
            proj[d, 2 * k, rows, :] = gate
            outbox[kind, pl.ds(4 * quad, 4)] = to_chans(gate * proj[d, 2 * k + 1, rows, :])

        return fill

    def out_gate(d):
        def fill(quad):
            rows = rows_of(quad)
            proj[d, 4, rows, :] = sigmoid(proj[d, 4, rows, :])

        all_quads(fill)

    def head_first(d):
        mean, inv = statistics(sums[d], 2 * d + 1)
        normalise(sums[d], mean, inv, 2 * d + 1, normed_sum)
        update[...] = product(weights_u[...], normed_sum[...])

    def backward_sums(source, x_ref, mean, inv, slot):
        keep_at = 2 * (slot % 2)

        zero = jnp.zeros((RB, COLS), F32)

        def fold(v):
            return v[:, 0:128] + v[:, 128:256] + v[:, 256:384] + v[:, 384:512]

        def body(step, carry):
            one, two = carry
            for k in range(4):
                c = 4 * step + k
                dn = source[pl.ds(pl.multiple_of(8 * c, 8), 8), :]
                standard = (x_ref[c].astype(F32) - mean) * inv
                scaled = dn * gain[slot, c]
                one = one + scaled
                two = two + scaled * standard
                partial[keep_at, c] = fold(dn * standard)
                partial[keep_at + 1, c] = fold(dn)
            return one, two

        one, two = lax.fori_loop(0, CH // 4, body, (zero, zero))
        return one * (1.0 / CH), two * (1.0 / CH)

    def small_sums(k):
        lane = lax.broadcasted_iota(jnp.int32, (CH, 128), 1)
        total = jnp.zeros((CH, 128), F32)
        for j in range(2):
            column = jnp.sum(jnp.sum(partial[2 * k + j], axis=1), axis=1, keepdims=True)
            total = total + jnp.where(lane == 2 * j + k, column, 0.0)
        return total

    def store_params(d, late, start, value, width):
        half, lane = start // 128, start % 128
        for block in range(8):
            param[d, block * 2 + half, late, :, lane : lane + width] = (
                value[block * 8 : block * 8 + 8, :]
            )

    def head_second(d, read_up):
        def gating(quad):
            rows = rows_of(quad)
            gated[rows, :] = (proj[d, 4, rows, :] * read_up(quad)).astype(BF16)

        all_quads(gating)
        work[...] = product(weights_d[...], gated[...])
        slot = 2 * d + 1
        mean, inv = stat[slot, 0], stat[slot, 1]
        one, two = backward_sums(work, sums[d], mean, inv, slot)

        def fill(quad):
            for k in range(4):
                c = 4 * quad + k
                dn = work[pl.ds(pl.multiple_of(8 * c, 8), 8), :]
                standard = (sums[d][c].astype(F32) - mean) * inv
                outbox[6 if d == 0 else 1, c] = (
                    inv * (dn * gain[slot, c] - one - standard * two)
                ).astype(BF16)

        return fill

    def gate_block(d, read_up):
        def body(quad):
            rows = rows_of(quad)
            gate = proj[d, 4, rows, :]
            d_gate = read_up(quad) * update[rows, :]
            d_proj[block_rows(4, quad), :] = (d_gate * gate * (1.0 - gate)).astype(BF16)

        all_quads(body)

    def spread_lanes(source, dest, start):
        moved = product(perm[...], source).astype(BF16)
        for r in range(RB):
            dest[start : start + CH, r * COLS : (r + 1) * COLS] = moved[r * CH : (r + 1) * CH, :]

    def head_params(d):
        spread_lanes(normed_sum[...], lanes_s, 0)
        spread_lanes(gated[...], lanes_r, 0)
        store_params(d, 0, 192, product(lanes_s[...], lanes_r[0:CH, :], ((1,), (1,))), CH)
        small[...] = small_sums(1)

    def tail_blocks(d, k):
        kind = (8 if d == 0 else 3) + k

        def body(quad):
            rows = rows_of(quad)
            grad = to_rows(inbox[kind, pl.ds(4 * quad, 4)])
            gate = proj[d, 2 * k, rows, :]
            value = proj[d, 2 * k + 1, rows, :]
            d_proj[block_rows(2 * k, quad), :] = (grad * value * gate * (1.0 - gate)).astype(BF16)
            d_proj[block_rows(2 * k + 1, quad), :] = (grad * gate).astype(BF16)

        all_quads(body)

    def tail_first(d):
        tail_blocks(d, 0)
        grad_n[...] = product(weights_q[:, 0:1024], d_proj[0:1024, :]) + product(
            weights_q[:, 2048:2560], d_proj[2048:2560, :]
        )

    def tail_second(d):
        tail_blocks(d, 1)
        grad_n[...] += product(weights_q[:, 1024:2048], d_proj[1024:2048, :])
        slot = 2 * d
        return backward_sums(grad_n, saved[d], stat[slot, 0], stat[slot, 1], slot)

    def tail_value(d, c, one, two):
        slot = 2 * d
        mean, inv = stat[slot, 0], stat[slot, 1]
        rows = pl.ds(pl.multiple_of(8 * c, 8), 8)
        standard = (saved[d][c].astype(F32) - mean) * inv
        return rows, inv * (grad_n[rows, :] * gain[slot, c] - one - standard * two)

    def early_params(d):
        spread_lanes(normed[d], lanes_n, 0)
        for at, b in enumerate((0, 1, 4)):
            spread_lanes(d_proj[b * ROWS : (b + 1) * ROWS, :], lanes_r, at * CH)
        value = product(lanes_n[...], lanes_r[0 : 3 * CH, :], ((1,), (1,)))
        store_params(d, 0, 0, value[:, 0:128], 128)
        store_params(d, 0, 128, value[:, 128:192], CH)

    def late_params(d):
        for at, b in enumerate((2, 3)):
            spread_lanes(d_proj[b * ROWS : (b + 1) * ROWS, :], lanes_r, at * CH)
        value = product(lanes_n[...], lanes_r[0 : 2 * CH, :], ((1,), (1,)))
        store_params(d, 1, 0, value, 128)
        store_params(d, 1, 128, small[...] + small_sums(0), 128)

    first = deep * 2 + core
    second = board * 8 + flat

    def to_first(d, member, source, dest, sem):
        pltpu.make_async_remote_copy(
            src_ref=source, dst_ref=dest,
            send_sem=send_sem.at[sem], recv_sem=recv_sem.at[sem],
            device_id={"tmpl": board * 2 + member % 2, "row": (member // 2) * 8 + flat},
            device_id_type=MESH,
        ).start()

    def sum_all(ref):
        total = ref[0]
        for k in range(1, HALF):
            total = total + ref[k]
        return total

    def sums_one(d):
        sem = 18 + 3 * d

        def body(step, carry):
            member = first ^ step
            to_first(d, member, param.at[d, member], recv_one.at[d, first], sem)
            return carry

        lax.fori_loop(1, HALF, body, 0)
        recv_one[d, first] = param[d, first]

    def sums_two(d):
        sem = 18 + 3 * d
        wait_recv(recv_one.at[d], sem, HALF - 1)
        part_sum[d, 0] = sum_all(recv_one.at[d])

        def body(step, carry):
            member = second ^ step
            pltpu.make_async_remote_copy(
                src_ref=part_sum.at[d, 0], dst_ref=recv_two.at[d, second],
                send_sem=send_sem.at[sem + 1], recv_sem=recv_sem.at[sem + 1],
                device_id={"tmpl": (member // 8) * 2 + core, "row": deep * 8 + member % 8},
                device_id_type=MESH,
            ).start()
            return carry

        lax.fori_loop(1, HALF, body, 0)
        recv_two[d, second] = part_sum[d, 0]

    def sums_three(d):
        sem = 18 + 3 * d
        wait_recv(recv_two.at[d], sem + 1, HALF - 1)
        part_sum[d, 1] = sum_all(recv_two.at[d]) * (1.0 / 2048.0)

        def body(step, carry):
            to_first(d, first ^ step, part_sum.at[d, 1], totals.at[d, first], sem + 2)
            return carry

        lax.fori_loop(1, HALF, body, 0)
        totals[d, first] = part_sum[d, 1]

    def load(kind, k):
        def body(quad):
            mats[k, rows_of(quad), :] = to_rows(inbox[kind, pl.ds(4 * quad, 4)]).astype(BF16)

        all_quads(body)

    def grad_fill(kind):
        def fill(quad):
            outbox[kind, pl.ds(4 * quad, 4)] = to_chans(work[rows_of(quad), :])

        return fill

    def read_cotangent(quad):
        return to_rows(cotangent[pl.ds(4 * quad, 4)])

    def read_upstream(quad):
        return upstream[rows_of(quad), :]

    build_forward(1, (2, 3))
    norm_input(1)
    project(1, (2, 3))
    pl.semaphore_wait(barrier, PEERS - 1 + 16)
    exchange(0, pair_fill(1, 1, 0))
    build_forward(1, (4,))
    build_output(1)
    project(1, (4,))
    out_gate(1)
    head_first(1)
    exchange(1, head_second(1, read_cotangent))
    build_forward(1, (0, 1))
    project(1, (0, 1))
    lane = lax.broadcasted_iota(jnp.int32, (ROWS, ROWS), 1)
    row = lax.broadcasted_iota(jnp.int32, (ROWS, ROWS), 0)
    perm[...] = jnp.where(lane == ((row & 63) << 3) + (row >> 6), 1.0, 0.0).astype(BF16)
    sent(0)
    exchange(2, pair_fill(1, 0, 2))
    gate_block(1, read_cotangent)
    head_params(1)
    build_backward(1)
    build_forward(0, (0, 1, 2, 3, 4))
    norm_input(0)

    arrived(0)
    arrived(1)
    load(0, 1)
    load(1, 2)
    work[...] = product(mats[1], mats[2], ((1,), (1,)))
    sent(1)
    exchange(3, grad_fill(3))
    project(0, (2, 3))
    arrived(2)
    load(2, 0)
    work[...] = product(mats[0], mats[2])
    sent(2)
    exchange(4, grad_fill(4))
    all_quads(pair_fill(0, 1, 5))
    project(0, (0, 1, 4))
    all_quads(pair_fill(0, 0, 7))
    out_gate(0)
    build_output(0)
    head_first(0)
    sent(3)
    exchange(5, None)

    arrived(3)
    tail_first(1)
    early_params(1)
    arrived(4)
    one, two = tail_second(1)

    def keep(quad):
        for k in range(4):
            c = 4 * quad + k
            rows, value = tail_value(1, c, one, two)
            upstream[rows, :] = cotangent[c].astype(F32) + value

    all_quads(keep)
    sent(4)
    exchange(6, head_second(0, read_upstream))
    late_params(1)
    gate_block(0, read_upstream)
    head_params(0)
    build_backward(0)
    sent(5)
    exchange(7, None)
    sums_one(1)

    arrived(5)
    arrived(6)
    load(5, 1)
    load(6, 2)
    work[...] = product(mats[2], mats[1])
    sent(6)
    exchange(8, grad_fill(8))
    arrived(7)
    load(7, 0)
    work[...] = product(mats[2], mats[0], ((0,), (0,)))
    sent(7)
    exchange(9, grad_fill(9))
    sums_two(1)
    arrived(8)
    tail_first(0)
    early_params(0)
    sums_three(1)
    arrived(9)
    one, two = tail_second(0)
    late_params(0)
    sums_one(0)

    for part in range(4):
        def spread(step, carry):
            for k in range(4):
                c = part * 16 + 4 * step + k
                rows, value = tail_value(0, c, one, two)
                value = upstream[rows, :] + value
                for t in range(4):
                    block = value[:, t * 128 : (t + 1) * 128]
                    result[t, c] = block
                    send_r[t, c] = block.astype(BF16)
            return carry

        lax.fori_loop(0, 4, spread, 0)
        chans = pl.ds(part * 16, 16)
        for hi in range(2):
            pltpu.make_async_remote_copy(
                src_ref=send_r.at[2 * hi + (1 - core), chans], dst_ref=recv_r.at[part, hi],
                send_sem=send_sem.at[10 + part], recv_sem=recv_sem.at[10 + part],
                device_id={"tmpl": board * 2 + (1 - core), "row": me}, device_id_type=MESH,
            ).start()
    sums_two(0)
    for part in range(4):
        chans = pl.ds(part * 16, 16)
        wait_recv(recv_r.at[part], 10 + part, 2)
        total = result[2 * (1 - board) + core, chans] + recv_r[part, 1 - board].astype(F32)
        send_h[part] = total.astype(BF16)
        pltpu.make_async_remote_copy(
            src_ref=send_h.at[part], dst_ref=recv_h.at[part],
            send_sem=send_sem.at[14 + part], recv_sem=recv_sem.at[14 + part],
            device_id={"tmpl": (1 - board) * 2 + core, "row": me}, device_id_type=MESH,
        ).start()
    sums_three(0)
    for part in range(4):
        chans = pl.ds(part * 16, 16)
        view = recv_h.at[part]
        pltpu.make_async_copy(view, view, recv_sem.at[14 + part]).wait()
        total = result[tm, chans] + recv_r[part, board].astype(F32) + recv_h[part].astype(F32)
        trunk[chans] = total.astype(BF16)
    for d in range(2):
        wait_recv(totals.at[d], 20 + 3 * d, HALF - 1)
    for kind in (8, 9):
        sent(kind)
    for part in range(4):
        wait_send(recv_r.at[part], 10 + part, 2)
        view = recv_h.at[part]
        pltpu.make_async_copy(view, view, send_sem.at[14 + part]).wait()
    for d in range(2):
        wait_send(recv_one.at[d], 18 + 3 * d, HALF - 1)
        wait_send(recv_two.at[d], 19 + 3 * d, HALF - 1)
        wait_send(totals.at[d], 20 + 3 * d, HALF - 1)


def unpack(trunk, totals, out, grad_in, grad_out, grad_gain, grad_shift):
    out[...] = trunk[...]
    for d in range(2):
        for block in range(8):
            rows = slice(block * 8, block * 8 + 8)
            left, right = totals[d, 2 * block], totals[d, 2 * block + 1]
            grad_in[d, rows, 0:128] = left[0]
            grad_in[d, rows, 128:256] = left[1]
            grad_in[d, rows, 256:320] = right[0, :, 0:64]
            grad_out[d, rows, :] = right[0, :, 64:128]
        small = [totals[d, 2 * block + 1, 1] for block in range(8)]
        small = jnp.concatenate(small + [jnp.zeros((CH, 128), F32)], 0).T
        grad_gain[d] = small[0:2, 0:CH]
        grad_shift[d] = small[2:4, 0:CH]


def shards(saved_out, sum_out, saved_in, sum_in, cotangent, w_in, w_out, norm_gain, norm_shift):
    vmem = pl.BlockSpec(memory_space=pltpu.VMEM)
    smem = pl.BlockSpec(memory_space=pltpu.SMEM)
    shape = jax.ShapeDtypeStruct
    full = (ROWS, COLS)
    boxes = (10, PEERS, RB, COLS)
    trunk, totals = pl.pallas_call(
        kernel,
        out_shape=(shape((CH, RB, 128), BF16), shape((2, HALF, 2, 8, 128), F32)),
        in_specs=[vmem] * 7 + [smem] * 2,
        out_specs=(vmem, vmem),
        scratch_shapes=[
            pltpu.VMEM((5 * ROWS, COLS), BF16),
            pltpu.VMEM((ROWS, 5 * COLS), BF16),
            pltpu.VMEM(full, BF16),
            pltpu.VMEM(full, BF16),
            pltpu.VMEM(full, BF16),
            pltpu.VMEM((2, ROWS, COLS), BF16),
            pltpu.VMEM(full, BF16),
            pltpu.VMEM(full, BF16),
            pltpu.VMEM((2, 5, ROWS, COLS), F32),
            pltpu.VMEM((4, 2, RB, COLS), F32),
            pltpu.VMEM(full, F32),
            pltpu.VMEM(full, F32),
            pltpu.VMEM(full, F32),
            pltpu.VMEM(full, F32),
            pltpu.VMEM((5 * ROWS, COLS), BF16),
            pltpu.VMEM((3, ROWS, COLS), BF16),
            pltpu.VMEM((4, CH, RB, 128), F32),
            pltpu.VMEM((CH, RB * COLS), BF16),
            pltpu.VMEM((CH, RB * COLS), BF16),
            pltpu.VMEM((3 * CH, RB * COLS), BF16),
            pltpu.VMEM((CH, 128), F32),
            pltpu.VMEM(boxes, BF16),
            pltpu.VMEM(boxes, BF16),
            pltpu.VMEM((4, CH, RB, 128), F32),
            pltpu.VMEM((4, CH, RB, 128), BF16),
            pltpu.VMEM((4, 2, 16, RB, 128), BF16),
            pltpu.VMEM((4, 16, RB, 128), BF16),
            pltpu.VMEM((4, 16, RB, 128), BF16),
            pltpu.VMEM((2, HALF, 2, 8, 128), F32),
            pltpu.VMEM((2, HALF, 2, 8, 128), F32),
            pltpu.VMEM((2, 2, 2, 8, 128), F32),
            pltpu.VMEM((2, HALF, 2, 8, 128), F32),
            pltpu.SemaphoreType.DMA((24,)),
            pltpu.SemaphoreType.DMA((24,)),
        ],
        compiler_params=pltpu.CompilerParams(
            collective_id=0, has_side_effects=True, vmem_limit_bytes=58 * 1024 * 1024
        ),
        name="triangle_backward",
    )(
        saved_out[0], sum_out[0], saved_in[0], sum_in[0], cotangent[0], w_in, w_out,
        norm_gain.reshape(4, CH), norm_shift.reshape(4, CH),
    )
    return pl.pallas_call(
        unpack,
        out_shape=(
            shape((CH, RB, 128), BF16), shape((2, CH, 5 * CH), F32), shape((2, CH, CH), F32),
            shape((2, 2, CH), F32), shape((2, 2, CH), F32),
        ),
        in_specs=[vmem] * 2,
        out_specs=(vmem,) * 5,
        name="unpack",
    )(trunk, totals)


def solution(mesh):
    whole = P("tmpl", None, "row", None)
    in_specs = (whole, whole, whole, whole, whole, P(), P(), P(), P())
    out_specs = (P(None, "row", "tmpl"), P(), P(), P(), P())
    return jax.shard_map(shards, mesh=mesh, in_specs=in_specs, out_specs=out_specs, check_vma=False)
```

time: 559 us -> 160 us (0.29); the launches traced: 551 us -> 160 us
  waiting for transfers between devices: 242 us -> 0 us
  Pallas kernels: 0 us -> 159 us
  starting transfers between devices: 101 us -> 0 us
  blocking collectives: 79.3 us -> 0 us
  other arithmetic: 50.3 us -> 0 us
  local copies, waits for them, and re-layouts: 37.8 us -> 0 us
  matrix products: 24.1 us -> 0 us
  between operations: 16.5 us -> 0.64 us
    psum x1 -> x0, waiting for transfers between devices: 162 us -> none  [shards(): summed = lax.psum(stacked, ('tmpl', 'row'))]
    pallas_call x0 -> x2, Pallas kernels: none -> 159 us  [the longest x1 158 us: shards(): pl.pallas_call(kernel, out_shape=(shape((CH, RB, 128), BF16), shape((2, H...]
    all_to_all x10 -> x0, starting transfers between devices: 101 us -> none  [the longest x2 19.4 us: send_back(): lax.all_to_all(grad_b, 'row', split_axis=1, concat_axis=0, tiled=True)]
    all_to_all x10 -> x0, waiting for transfers between devices: 79.6 us -> none  [the longest x1 13.6 us: shards(): lax.all_to_all(head_in[0], 'row', split_axis=0, concat_axis=1, tiled=True)]
    psum x1 -> x0, blocking collectives: 79.3 us -> none  [shards(): summed = lax.psum(stacked, ('tmpl', 'row'))]
    unnamed x15 -> x0, other arithmetic: 27.8 us -> none
    unnamed x59 -> x0, local copies, waits for them, and re-layouts: 26.1 us -> none
    dot_general x16 -> x0, matrix products: 24.1 us -> none  [the longest x2 5.43 us: prepare(): jnp.einsum('cf,crn->frn', weight_in, normed_b, preferred_element_type=jnp...]
  transfers between devices with their start and end apart: 12 -> 0, of which waited for: 11 -> 0; matrix products, arithmetic and copies ran while one was open for 13% -> 0% of each run, Pallas kernels for 0% -> 0%
where the time goes in v2:
time: 160 us
  Pallas kernels  159 us (99%)
    pallas_call x1, Pallas kernels, shards(): pl.pallas_call(kernel, out_shape=(shape((CH, RB, 128), BF16), shape((2, H...  158 us

profile of v2, /device:TPU:1, one launch (start us, length us, event | category | flops | bytes accessed | tf_op | source)
XLA Modules:
  0.0 160.1 jit_solution(11322364791137018524)
XLA Ops:
  0.6 157.7 %triangle_backward.1 = (bf16[64,8,128]{2,1,0:T(8,128)(2,1)}, f32[2,16,2,8,128]{4,3,2,1,0:T(8,128)}) custom-call(bf16[64,8,512]{2,1,0:T(8,128)(2,1)} %bitcast.7, bf16[64,8,512]{2,1,0:T(8,128)(2,1)} %bitcast.8, bf16[64,8,512]{2,1,0:T(8,128)(2,1)} %bitcast.9, bf16[64,8,512]{2,1,0:T(8,128)(2,1)} %bitcast.10, bf16[64,8,512]{2,1,0:T(8,128)(2,1)} %bitcast.11, ...), custom_call_target="tpu_custom_call" | custom-call | tf_op jit(solution)/shard_map/triangle_backward/pallas_call | solution.py:593
  158.3 1.8 %unpack.1 = (bf16[64,8,128]{2,1,0:T(8,128)(2,1)}, f32[2,64,320]{2,1,0:T(8,128)}, f32[2,64,64]{2,1,0:T(8,128)}, f32[2,2,64]{2,1,0:T(2,128)}, f32[2,2,64]{2,1,0:T(2,128)}) custom-call(bf16[64,8,128]{2,1,0:T(8,128)(2,1)} %get-tuple-element.7.trunk, f32[2,16,2,8,128]{4,3,2,1,0:T(8,128)} %get-tuple-element.8.totals), custom_call_target="tpu_custom_call" | custom-call | tf_op jit(solution)/shard_map/unpack/pallas_call | solution.py:642

commit v3 on v2

--- a/solution.py
+++ b/solution.py
@@ -76,42 +76,58 @@
     def to_chans(values):
         return values.reshape(4, RB, COLS).astype(BF16)
 
-    def expand_rows(table, dest, top, start):
+    def halves(step):
+        return pl.ds(pl.multiple_of((step % 2) * 256, 256), 256)
+
+    def multiply(dest, left, right, flip=False):
+        def body(step, carry):
+            if flip:
+                dest[:, halves(step)] = product(left[...], right[halves(step), :], ((1,), (1,)))
+            else:
+                dest[:, halves(step)] = product(left[...], right[:, halves(step)])
+            return carry
+
+        lax.fori_loop(0, 2, body, 0)
+
+    def expand_rows(dest, top, count):
         lane = lax.broadcasted_iota(jnp.int32, (RB, COLS), 1)
         row = lax.broadcasted_iota(jnp.int32, (RB, COLS), 0)
         mask = jnp.where((lane & 7) == row, 1.0, 0.0).astype(F32)
-        work[0:CH, :] = table
 
         def body(step, carry):
             block = work[pl.ds(pl.multiple_of(8 * step, 8), 8), :]
             parts = [block[k : k + 1, :] * mask for k in range(8)]
             at = pl.multiple_of(top + 64 * step, 64)
-            dest[pl.ds(at, 64), start : start + COLS] = jnp.concatenate(parts, 0).astype(BF16)
-            return carry
-
-        lax.fori_loop(0, CH // 8, body, 0)
+            dest[pl.ds(at, 64), :] = jnp.concatenate(parts, 0).astype(BF16)
+            return carry
+
+        lax.fori_loop(0, count * CH // 8, body, 0)
 
     def one_hot():
         lane = lax.broadcasted_iota(jnp.int32, (CH, COLS), 1)
         row = lax.broadcasted_iota(jnp.int32, (CH, COLS), 0)
         return jnp.where((lane >> 3) == row, 1.0, 0.0).astype(BF16)
 
-    def build_forward(d, blocks):
+    def build_forward(d, low, count):
         spread = one_hot()
-        for b in blocks:
+        for b in range(low, low + count):
             table = product(w_in[d, :, b * CH : (b + 1) * CH], spread, ((0,), (0,)))
-            expand_rows(table, weights_p, b * ROWS, 0)
+            work[(b - low) * CH : (b - low + 1) * CH, :] = table
+        expand_rows(weights_p, low * ROWS, count)
 
     def build_backward(d):
         spread = one_hot()
         for b in range(5):
             table = product(w_in[d, :, b * CH : (b + 1) * CH], spread)
-            expand_rows(table, weights_q, 0, b * COLS)
+            work[b * CH : (b + 1) * CH, :] = table
+        expand_rows(weights_q, d * 5 * ROWS, 5)
 
     def build_output(d):
         spread = one_hot()
-        expand_rows(product(w_out[d], spread, ((0,), (0,))), weights_u, 0, 0)
-        expand_rows(product(w_out[d], spread), weights_d, 0, 0)
+        work[0:CH, :] = product(w_out[d], spread, ((0,), (0,)))
+        expand_rows(weights_u, 0, 1)
+        work[0:CH, :] = product(w_out[d], spread)
+        expand_rows(weights_d, 0, 1)
 
     def statistics(x_ref, slot):
         zero = jnp.zeros((RB, COLS), F32)
@@ -192,9 +208,14 @@
     def sent(kind):
         wait_send(inbox.at[kind], kind, PEERS - 1)
 
-    def project(d, blocks):
-        for b in blocks:
-            proj[d, b] = product(weights_p[b * ROWS : (b + 1) * ROWS, :], normed[d])
+    def project(d, low, count):
+        def body(step, carry):
+            block = low + step // 2
+            left = weights_p[pl.ds(pl.multiple_of(block * ROWS, ROWS), ROWS), :]
+            proj[d, block, :, halves(step)] = product(left, normed[d, :, halves(step)])
+            return carry
+
+        lax.fori_loop(0, 2 * count, body, 0)
 
     def norm_input(d):
         mean, inv = statistics(saved[d], 2 * d)
@@ -219,7 +240,7 @@
     def head_first(d):
         mean, inv = statistics(sums[d], 2 * d + 1)
         normalise(sums[d], mean, inv, 2 * d + 1, normed_sum)
-        update[...] = product(weights_u[...], normed_sum[...])
+        multiply(update, weights_u, normed_sum)
 
     def backward_sums(source, x_ref, mean, inv, slot):
         keep_at = 2 * (slot % 2)
@@ -266,7 +287,7 @@
             gated[rows, :] = (proj[d, 4, rows, :] * read_up(quad)).astype(BF16)
 
         all_quads(gating)
-        work[...] = product(weights_d[...], gated[...])
+        multiply(work, weights_d, gated)
         slot = 2 * d + 1
         mean, inv = stat[slot, 0], stat[slot, 1]
         one, two = backward_sums(work, sums[d], mean, inv, slot)
@@ -291,15 +312,32 @@
 
         all_quads(body)
 
-    def spread_lanes(source, dest, start):
-        moved = product(perm[...], source).astype(BF16)
-        for r in range(RB):
-            dest[start : start + CH, r * COLS : (r + 1) * COLS] = moved[r * CH : (r + 1) * CH, :]
+    def spread_lanes(source, dest, count, place):
+        def body(step, carry):
+            at = place(step // 2)
+            moved = product(perm[...], source[pl.ds(at, ROWS), halves(step)]).astype(BF16)
+            rows = pl.ds(pl.multiple_of((step // 2) * CH, CH), CH)
+            for r in range(RB):
+                lanes = pl.ds(pl.multiple_of(r * COLS + (step % 2) * 256, 256), 256)
+                dest[rows, lanes] = moved[r * CH : (r + 1) * CH, :]
+            return carry
+
+        lax.fori_loop(0, 2 * count, body, 0)
+
+    def gram(left, count):
+        def body(step, total):
+            lanes = pl.ds(pl.multiple_of(step * COLS, COLS), COLS)
+            return total + product(left[:, lanes], lanes_r[0 : count * CH, lanes], ((1,), (1,)))
+
+        return lax.fori_loop(0, RB, body, jnp.zeros((CH, count * CH), F32))
+
+    def whole(step):
+        return 0
 
     def head_params(d):
-        spread_lanes(normed_sum[...], lanes_s, 0)
-        spread_lanes(gated[...], lanes_r, 0)
-        store_params(d, 0, 192, product(lanes_s[...], lanes_r[0:CH, :], ((1,), (1,))), CH)
+        spread_lanes(normed_sum, lanes_s, 1, whole)
+        spread_lanes(gated, lanes_r, 1, whole)
+        store_params(d, 0, 192, gram(lanes_s, 1), CH)
         small[...] = small_sums(1)
 
     def tail_blocks(d, k):
@@ -315,15 +353,32 @@
 
         all_quads(body)
 
+    def add_blocks(d, count, place, fresh):
+        def body(step, carry):
+            at = place(step // 2)
+            rows = pl.ds(at, ROWS)
+            left = weights_q[pl.ds(d * 5 * ROWS + at, ROWS), :]
+            value = product(left, d_proj[rows, halves(step)])
+            grad_n[:, halves(step)] += value
+            return carry
+
+        if fresh:
+            grad_n[...] = jnp.zeros((ROWS, COLS), F32)
+        lax.fori_loop(0, 2 * count, body, 0)
+
+    def early_place(step):
+        return pl.multiple_of((step + 2 * (step // 2)) * ROWS, ROWS)
+
+    def late_place(step):
+        return pl.multiple_of((step + 2) * ROWS, ROWS)
+
     def tail_first(d):
         tail_blocks(d, 0)
-        grad_n[...] = product(weights_q[:, 0:1024], d_proj[0:1024, :]) + product(
-            weights_q[:, 2048:2560], d_proj[2048:2560, :]
-        )
+        add_blocks(d, 3, early_place, True)
 
     def tail_second(d):
         tail_blocks(d, 1)
-        grad_n[...] += product(weights_q[:, 1024:2048], d_proj[1024:2048, :])
+        add_blocks(d, 2, late_place, False)
         slot = 2 * d
         return backward_sums(grad_n, saved[d], stat[slot, 0], stat[slot, 1], slot)
 
@@ -335,18 +390,15 @@
         return rows, inv * (grad_n[rows, :] * gain[slot, c] - one - standard * two)
 
     def early_params(d):
-        spread_lanes(normed[d], lanes_n, 0)
-        for at, b in enumerate((0, 1, 4)):
-            spread_lanes(d_proj[b * ROWS : (b + 1) * ROWS, :], lanes_r, at * CH)
-        value = product(lanes_n[...], lanes_r[0 : 3 * CH, :], ((1,), (1,)))
+        spread_lanes(normed.at[d], lanes_n, 1, whole)
+        spread_lanes(d_proj, lanes_r, 3, early_place)
+        value = gram(lanes_n, 3)
         store_params(d, 0, 0, value[:, 0:128], 128)
         store_params(d, 0, 128, value[:, 128:192], CH)
 
     def late_params(d):
-        for at, b in enumerate((2, 3)):
-            spread_lanes(d_proj[b * ROWS : (b + 1) * ROWS, :], lanes_r, at * CH)
-        value = product(lanes_n[...], lanes_r[0 : 2 * CH, :], ((1,), (1,)))
-        store_params(d, 1, 0, value, 128)
+        spread_lanes(d_proj, lanes_r, 2, late_place)
+        store_params(d, 1, 0, gram(lanes_n, 2), 128)
         store_params(d, 1, 128, small[...] + small_sums(0), 128)
 
     first = deep * 2 + core
@@ -425,19 +477,19 @@
     def read_upstream(quad):
         return upstream[rows_of(quad), :]
 
-    build_forward(1, (2, 3))
+    build_forward(1, 2, 2)
     norm_input(1)
-    project(1, (2, 3))
+    project(1, 2, 2)
     pl.semaphore_wait(barrier, PEERS - 1 + 16)
     exchange(0, pair_fill(1, 1, 0))
-    build_forward(1, (4,))
+    build_forward(1, 4, 1)
     build_output(1)
-    project(1, (4,))
+    project(1, 4, 1)
     out_gate(1)
     head_first(1)
     exchange(1, head_second(1, read_cotangent))
-    build_forward(1, (0, 1))
-    project(1, (0, 1))
+    build_forward(1, 0, 2)
+    project(1, 0, 2)
     lane = lax.broadcasted_iota(jnp.int32, (ROWS, ROWS), 1)
     row = lax.broadcasted_iota(jnp.int32, (ROWS, ROWS), 0)
     perm[...] = jnp.where(lane == ((row & 63) << 3) + (row >> 6), 1.0, 0.0).astype(BF16)
@@ -446,30 +498,32 @@
     gate_block(1, read_cotangent)
     head_params(1)
     build_backward(1)
-    build_forward(0, (0, 1, 2, 3, 4))
+    build_forward(0, 0, 5)
     norm_input(0)
+    project(0, 0, 5)
+    all_quads(pair_fill(0, 1, 5))
+    sent(1)
+    exchange(5, None)
 
     arrived(0)
     arrived(1)
     load(0, 1)
     load(1, 2)
-    work[...] = product(mats[1], mats[2], ((1,), (1,)))
-    sent(1)
+    multiply(work, mats.at[1], mats.at[2], True)
     exchange(3, grad_fill(3))
-    project(0, (2, 3))
     arrived(2)
     load(2, 0)
-    work[...] = product(mats[0], mats[2])
+    multiply(work, mats.at[0], mats.at[2])
     sent(2)
     exchange(4, grad_fill(4))
-    all_quads(pair_fill(0, 1, 5))
-    project(0, (0, 1, 4))
     all_quads(pair_fill(0, 0, 7))
+    exchange(7, None)
     out_gate(0)
     build_output(0)
     head_first(0)
+    build_backward(0)
+    sent(5)
     sent(3)
-    exchange(5, None)
 
     arrived(3)
     tail_first(1)
@@ -487,26 +541,22 @@
     sent(4)
     exchange(6, head_second(0, read_upstream))
     late_params(1)
+    sums_one(1)
+    arrived(5)
+    arrived(7)
+    load(5, 1)
+    load(7, 0)
+    arrived(6)
+    load(6, 2)
+    multiply(work, mats.at[2], mats.at[1])
+    sent(7)
+    exchange(8, grad_fill(8))
+    work[...] = product(mats[2], mats[0], ((0,), (0,)))
+    sent(6)
+    exchange(9, grad_fill(9))
+    sums_two(1)
     gate_block(0, read_upstream)
     head_params(0)
-    build_backward(0)
-    sent(5)
-    exchange(7, None)
-    sums_one(1)
-
-    arrived(5)
-    arrived(6)
-    load(5, 1)
-    load(6, 2)
-    work[...] = product(mats[2], mats[1])
-    sent(6)
-    exchange(8, grad_fill(8))
-    arrived(7)
-    load(7, 0)
-    work[...] = product(mats[2], mats[0], ((0,), (0,)))
-    sent(7)
-    exchange(9, grad_fill(9))
-    sums_two(1)
     arrived(8)
     tail_first(0)
     early_params(0)
@@ -597,7 +647,7 @@
         out_specs=(vmem, vmem),
         scratch_shapes=[
             pltpu.VMEM((5 * ROWS, COLS), BF16),
-            pltpu.VMEM((ROWS, 5 * COLS), BF16),
+            pltpu.VMEM((10 * ROWS, COLS), BF16),
             pltpu.VMEM(full, BF16),
             pltpu.VMEM(full, BF16),
             pltpu.VMEM(full, BF16),

time: 160 us -> 165 us (1.031)
  Pallas kernels: 159 us -> 164 us
    pallas_call x1, Pallas kernels: 158 us -> 163 us  [shards(): pl.pallas_call(kernel, out_shape=(shape((CH, RB, 128), BF16), shape((2, H...]
where the time goes in v3:
time: 165 us
  Pallas kernels  164 us (99%)
    pallas_call x1, Pallas kernels, shards(): pl.pallas_call(kernel, out_shape=(shape((CH, RB, 128), BF16), shape((2, H...  163 us

profile of v3, /device:TPU:1, one launch (start us, length us, event | category | flops | bytes accessed | tf_op | source)
XLA Modules:
  0.0 165.1 jit_solution(17202653512028477577)
XLA Ops:
  0.6 162.7 %triangle_backward.1 = (bf16[64,8,128]{2,1,0:T(8,128)(2,1)}, f32[2,16,2,8,128]{4,3,2,1,0:T(8,128)}) custom-call(bf16[64,8,512]{2,1,0:T(8,128)(2,1)} %bitcast.7, bf16[64,8,512]{2,1,0:T(8,128)(2,1)} %bitcast.8, bf16[64,8,512]{2,1,0:T(8,128)(2,1)} %bitcast.9, bf16[64,8,512]{2,1,0:T(8,128)(2,1)} %bitcast.10, bf16[64,8,512]{2,1,0:T(8,128)(2,1)} %bitcast.11, ...), custom_call_target="tpu_custom_call" | custom-call | tf_op jit(solution)/shard_map/triangle_backward/pallas_call | solution.py:643
  163.3 1.8 %unpack.1 = (bf16[64,8,128]{2,1,0:T(8,128)(2,1)}, f32[2,64,320]{2,1,0:T(8,128)}, f32[2,64,64]{2,1,0:T(8,128)}, f32[2,2,64]{2,1,0:T(2,128)}, f32[2,2,64]{2,1,0:T(2,128)}) custom-call(bf16[64,8,128]{2,1,0:T(8,128)(2,1)} %get-tuple-element.7.trunk, f32[2,16,2,8,128]{4,3,2,1,0:T(8,128)} %get-tuple-element.8.totals), custom_call_target="tpu_custom_call" | custom-call | tf_op jit(solution)/shard_map/unpack/pallas_call | solution.py:692

commit v4 on v2

--- a/solution.py
+++ b/solution.py
@@ -486,13 +486,10 @@
     all_quads(keep)
     sent(4)
     exchange(6, head_second(0, read_upstream))
-    late_params(1)
+    exchange(7, None)
     gate_block(0, read_upstream)
-    head_params(0)
     build_backward(0)
     sent(5)
-    exchange(7, None)
-    sums_one(1)
 
     arrived(5)
     arrived(6)
@@ -506,15 +503,18 @@
     work[...] = product(mats[2], mats[0], ((0,), (0,)))
     sent(7)
     exchange(9, grad_fill(9))
-    sums_two(1)
+    late_params(1)
+    sums_one(1)
+    head_params(0)
     arrived(8)
     tail_first(0)
     early_params(0)
-    sums_three(1)
+    sums_two(1)
     arrived(9)
     one, two = tail_second(0)
     late_params(0)
     sums_one(0)
+    sums_three(1)
 
     for part in range(4):
         def spread(step, carry):

time: 160 us -> 159 us (level)
  no operation moved by 1% of the time
where the time goes in v4:
time: 159 us
  Pallas kernels  158 us (99%)
    pallas_call x1, Pallas kernels, shards(): pl.pallas_call(kernel, out_shape=(shape((CH, RB, 128), BF16), shape((2, H...  156 us

profile of v4, /device:TPU:1, one launch (start us, length us, event | category | flops | bytes accessed | tf_op | source)
XLA Modules:
  0.0 158.9 jit_solution(1650296177780669976)
XLA Ops:
  0.6 156.5 %triangle_backward.1 = (bf16[64,8,128]{2,1,0:T(8,128)(2,1)}, f32[2,16,2,8,128]{4,3,2,1,0:T(8,128)}) custom-call(bf16[64,8,512]{2,1,0:T(8,128)(2,1)} %bitcast.7, bf16[64,8,512]{2,1,0:T(8,128)(2,1)} %bitcast.8, bf16[64,8,512]{2,1,0:T(8,128)(2,1)} %bitcast.9, bf16[64,8,512]{2,1,0:T(8,128)(2,1)} %bitcast.10, bf16[64,8,512]{2,1,0:T(8,128)(2,1)} %bitcast.11, ...), custom_call_target="tpu_custom_call" | custom-call | tf_op jit(solution)/shard_map/triangle_backward/pallas_call | solution.py:593
  157.1 1.8 %unpack.1 = (bf16[64,8,128]{2,1,0:T(8,128)(2,1)}, f32[2,64,320]{2,1,0:T(8,128)}, f32[2,64,64]{2,1,0:T(8,128)}, f32[2,2,64]{2,1,0:T(2,128)}, f32[2,2,64]{2,1,0:T(2,128)}) custom-call(bf16[64,8,128]{2,1,0:T(8,128)(2,1)} %get-tuple-element.7.trunk, f32[2,16,2,8,128]{4,3,2,1,0:T(8,128)} %get-tuple-element.8.totals), custom_call_target="tpu_custom_call" | custom-call | tf_op jit(solution)/shard_map/unpack/pallas_call | solution.py:642
